TPU v7x, 32 devices: a whole 2x2x4 slice. The times are simulated.
32 devices in a mesh: row: 2 (over core), col: 16 (over z, y, x).
Axes of the slice: x: 2, y: 2, z: 4, core: 2. Of those that a mesh axis runs over, the one named last changes fastest.
Arguments:
- features: bfloat16 [4096, 128], P(('row', 'col')), may hold values from -6 to 6
- weight: bfloat16 [128, 512], replicated, may hold values from -0.5 to 0.5
- bias: float32 [512], replicated, may hold values from -4 to 4
- tile_values: bfloat16 [2, 16, 16, 128, 128], P('row', 'col'), may hold values from 0 to 0.019897461
- tile_index: int32 [2, 16, 16], P('row', 'col'), may hold values from 0 to 31, as said below
- tile_count: int32 [2, 16], P('row', 'col'), may hold values from 2 to 16, as said below
- cotangent: bfloat16 [4096, 512], P(('col', 'row')), may hold values from -20 to 20
Outputs:
- hidden_out: bfloat16 [4096, 512], P(('col', 'row'))
- grad_features: bfloat16 [4096, 128], P(('row', 'col'))
- grad_weight: float32 [128, 512], replicated
- grad_bias: float32 [512], replicated
Inputs may be any that keep to these rules, and one draw needn't show every extreme that they name: `tile_index`: within a cell the slots name distinct tiles; slots at or beyond the cell's count hold arbitrary tiles and values. `tile_count`: counts differ from cell to cell; some cell holds exactly 16 live slots.
All inputs are finite; a program needn't handle non-finite values.
Results may differ from a plain program's by a relative error of at most 0.0065.
Values may be sent and summed in bfloat16 or wider, within the bound.
A program may use at most 128 MiB of HBM per device.

v0:
```python
import jax
import jax.numpy as jnp
from jax import lax
from jax.sharding import PartitionSpec as P


def tile_products(tiles, take_idx, put_idx, live, source, count_out):
    slots = tiles.shape[0]
    block = 16
    width = source.shape[-1]
    size = tiles.shape[-1]
    widened = source.dtype == jnp.float32

    def step(turn, acc):
        begin = turn * block
        part_tiles = lax.dynamic_slice_in_dim(tiles, begin, block, 0)
        part_take = lax.dynamic_slice_in_dim(take_idx, begin, block, 0)
        part_put = lax.dynamic_slice_in_dim(put_idx, begin, block, 0)
        part_live = lax.dynamic_slice_in_dim(live, begin, block, 0)
        picked = jnp.take(source, part_take, axis=0)
        onehot = (
            (part_put[None, :] == jnp.arange(count_out, dtype=jnp.int32)[:, None])
            & part_live[None, :]
        ).astype(jnp.float32)
        if widened:
            prod = jnp.einsum(
                "kab,kbh->kah",
                part_tiles.astype(jnp.float32),
                picked,
                precision=lax.Precision.HIGHEST,
            )
            return acc + jnp.einsum("tk,kah->tah", onehot, prod, precision=lax.Precision.HIGHEST)
        prod = jnp.einsum("kab,kah->kbh", part_tiles, picked, preferred_element_type=jnp.float32)
        return acc + jnp.einsum("tk,kah->tah", onehot, prod, precision=lax.Precision.HIGHEST)

    start = jnp.zeros((count_out, size, width), jnp.float32)
    return lax.fori_loop(0, slots // block, step, start)


def local(features, weight, bias, tile_values, tile_index, tile_count, cotangent):
    tiles = tile_values[0, 0]
    size = tiles.shape[-1]
    width = weight.shape[1]
    places = tile_index[0, 0]
    slots = jnp.arange(tiles.shape[0], dtype=jnp.int32)
    live = slots < tile_count[0, 0]
    weight_wide = weight.astype(jnp.float32)
    source_block = lax.all_gather(features, "col", axis=0, tiled=True)
    tile_cols = source_block.shape[0] // size
    tile_rows = cotangent.shape[0] * lax.axis_size("row") // size
    projected = jnp.dot(source_block, weight, preferred_element_type=jnp.float32)
    partial_value = tile_products(
        tiles,
        places % tile_cols,
        places // tile_cols,
        live,
        projected.reshape(tile_cols, size, width),
        tile_rows,
    )
    pre = (
        lax.psum_scatter(
            partial_value.reshape(tile_rows * size, width), "row", scatter_dimension=0, tiled=True
        )
        + bias[None, :]
    )
    hidden_out = jax.nn.silu(pre).astype(jnp.bfloat16)
    sig = jax.nn.sigmoid(pre)
    dpre = (cotangent.astype(jnp.float32) * (sig + pre * sig * (1.0 - sig))).astype(jnp.bfloat16)
    bias_part = jnp.sum(dpre.astype(jnp.float32), axis=0)
    grad_bias = lax.psum(bias_part, ("row", "col"))
    target_block = lax.all_gather(dpre, "row", axis=0, tiled=True)
    dproj_part = tile_products(
        tiles,
        places // tile_cols,
        places % tile_cols,
        live,
        target_block.reshape(tile_rows, size, width),
        tile_cols,
    )
    dproj_part = dproj_part.reshape(tile_cols * size, width)
    dproj = lax.psum_scatter(dproj_part, "col", scatter_dimension=0, tiled=True)
    grad_features = jnp.dot(dproj, weight_wide.T, precision=lax.Precision.HIGHEST).astype(
        jnp.bfloat16
    )
    weight_part = jnp.dot(features.astype(jnp.float32).T, dproj, precision=lax.Precision.HIGHEST)
    grad_weight = lax.psum(weight_part, ("row", "col"))
    return (hidden_out, grad_features, grad_weight, grad_bias)


def solution(mesh):
    in_specs = (
        P(("row", "col"), None),
        P(),
        P(),
        P("row", "col", None, None, None),
        P("row", "col", None),
        P("row", "col"),
        P(("col", "row"), None),
    )
    out_specs = (P(("col", "row"), None), P(("row", "col"), None), P(), P())
    return jax.shard_map(local, mesh=mesh, in_specs=in_specs, out_specs=out_specs, check_vma=False)
```

profile of v0, /device:TPU:0, one launch (start us, length us, event | category | flops | bytes accessed | tf_op | source)
XLA Modules:
  0.0 344.0 jit_solution(12262439195842870511)
XLA Ops:
  7.2 0.0 copy-start
  7.2 0.0 reduce-scatter.3.cloned.1.call-start
  7.9 0.7 fusion.26
  8.6 0.7 compare_and_fusion
  9.3 45.6 %all_gather.6 = bf16[2048,128]{1,0:T(8,128)(2,1)S(1)} all-gather(bf16[128,128]{1,0:T(8,128)(2,1)} %param.7), channel_id=1, replica_groups=mesh['row'=2,'col'=16] {'col'}, dimensions={0}, use_global_device_ids=true | all-gather | bytes 557056 | tf_op jit(solution)/shard_map/all_gather | solution.py:48
  54.8 3.6 %fusion.30 = f32[2048,512]{1,0:T(8,128)} fusion(bf16[2048,128]{1,0:T(8,128)(2,1)S(1)} %all_gather.6, bf16[128,512]{1,0:T(8,128)(2,1)} %param.8), kind=kOutput, calls=%fused_computation.59 | convolution fusion | flops 268435456 | bytes 4849664 | tf_op jit(solution)/shard_map/dot_general | solution.py:51
  58.4 4.9 %gather_fusion = f32[16,128,512]{2,1,0:T(8,128)} fusion(f32[16,128,512]{2,1,0:T(8,128)} %bitcast.71, s32[1024]{0:T(1024)S(1)} %pad_clamp_fusion.1), kind=kCustom, calls=%fused_computation | custom fusion | bytes 8388672 | tf_op jit(solution)/shard_map/while/body/eval_jaxpr/jit(_take)/gather | solution.py:20
  63.3 0.0 copy-done
  63.3 7.7 %fusion.4 = f32[16,512,128]{2,1,0:T(8,128)} fusion(f32[16,128,512]{2,1,0:T(8,128)} %gather_fusion, pred[16]{0:T(512)(128)(4,1)S(1)} %get-tuple-element.69, bf16[1,1,16,128,128]{4,3,2,1,0:T(8,128)(2,1)S(1)} %copy-done), kind=kOutput, calls=%fused_computation.6 | convolution fusion | flops 1611661312 | bytes 8912912 | tf_op jit(solution)/shard_map/while/body/eval_jaxpr/kab,kbh->kah/dot_general | solution.py:26
  71.0 5.5 %copy.15 = f32[16,512,128]{1,0,2:T(8,128)} copy(f32[16,512,128]{2,1,0:T(8,128)} %fusion.4) | data formatting | bytes 8388608 | tf_op jit(solution)/shard_map/while/body/eval_jaxpr/kab,kbh->kah/dot_general | solution.py:26
  76.5 0.0 copy-start.2
  76.5 0.0 copy-start.4
  76.5 3.8 %fusion.2 = f32[2,128,512]{2,0,1:T(2,128)S(1)} fusion(f32[16,512,128]{1,0,2:T(8,128)} %copy.15, pred[16]{0:T(512)(128)(4,1)S(1)} %get-tuple-element.71, s32[16]{0:T(128)S(1)} %get-tuple-element.55), kind=kOutput, calls=%fused_computation.4 | convolution fusion | flops 25165888 | bytes 4718672 | tf_op jit(solution)/shard_map/while/body/eval_jaxpr/tk,kah->tah/dot_general | solution.py:32
  80.3 0.9 copy.12
  81.2 0.0 reduce-scatter.3.cloned.1.call-update
  81.2 0.0 reduce-scatter.5.cloned.1.call-start
  81.3 3.9 %reduce-scatter.3.cloned.1.call-done = f32[128,512]{1,0:T(8,128)} async-done(((f32[256,512]{1,0:T(8,128)}), f32[128,512]{1,0:T(8,128)}) %reduce-scatter.3.cloned.1.call-update) | async-done | bytes 262160 | tf_op jit(solution)/shard_map/reduce_scatter | solution.py:61
  85.2 0.0 copy-done.2
  85.2 0.0 copy-done.4
  85.2 1.7 convert_reduce_fusion
  87.0 2.2 all_gather.7
  89.1 0.7 gather_fusion.1
  89.8 2.8 fusion.6
  92.6 5.5 %copy.16 = f32[16,512,128]{1,0,2:T(8,128)} copy(f32[16,512,128]{2,1,0:T(8,128)} %fusion.6) | data formatting | bytes 8388608 | tf_op jit(solution)/shard_map/while/body/eval_jaxpr/kab,kah->kbh/dot_general | solution.py:33
  98.1 4.3 %fusion = f32[16,128,512]{2,0,1:T(8,128)S(1)} fusion(f32[16,512,128]{1,0,2:T(8,128)} %copy.16, s32[16]{0:T(128)S(1)} %get-tuple-element.70, pred[16]{0:T(512)(128)(4,1)S(1)} %get-tuple-element.71), kind=kOutput, calls=%fused_computation.2 | convolution fusion | flops 201327104 | bytes 8388688 | tf_op jit(solution)/shard_map/while/body/eval_jaxpr/tk,kah->tah/dot_general | solution.py:34
  102.4 4.4 %copy.13 = f32[16,128,512]{2,1,0:T(8,128)} copy(f32[16,128,512]{2,0,1:T(8,128)S(1)} %fusion) | data formatting | bytes 8388608 | tf_op jit(solution)/shard_map/while/body/eval_jaxpr/tk,kah->tah/dot_general | solution.py:34
  106.8 0.0 copy-start.3
  106.8 0.0 copy-start.1
  106.8 0.0 reduce-scatter.5.cloned.1.call-update
  106.8 0.0 all-reduce.2.cloned.1.call-start
  106.9 45.7 %psum.15 = f32[512]{0:T(512)} all-reduce(f32[512]{0:T(512)S(1)} %get-tuple-element.52), channel_id=1, replica_groups=mesh['row'=2,'col'=16] {'row','col'}, use_global_device_ids=true, to_apply=%region_4.5 | all-reduce | flops 512 | bytes 4096 | tf_op jit(solution)/shard_map/psum | solution.py:70
  152.6 51.5 %reduce-scatter.5.cloned.1.call-done = f32[128,512]{1,0:T(8,128)} async-done(((f32[2048,512]{1,0:T(8,128)}), f32[128,512]{1,0:T(8,128)}) %reduce-scatter.5.cloned.1.call-update) | async-done | bytes 262160 | tf_op jit(solution)/shard_map/reduce_scatter | solution.py:81
  204.1 0.0 copy-done.3
  204.1 2.0 convolution_bitcast_fusion
  206.1 0.0 all-reduce.2.cloned.1.call-update
  206.1 0.0 copy-done.1
  206.1 1.8 convolution_convert_fusion
  208.0 127.7 %all-reduce.2.cloned.1.call-done = f32[128,512]{0,1:T(8,128)} async-done(((f32[128,512]{0,1:T(8,128)}), f32[128,512]{0,1:T(8,128)}) %all-reduce.2.cloned.1.call-update) | async-done | bytes 262160 | tf_op jit(solution)/shard_map/psum | solution.py:86
  335.7 1.8 copy.14
  (2 shorter events, 0.0 us)
Async XLA Ops:
  7.2 56.2 %copy-start = (bf16[1,1,16,128,128]{4,3,2,1,0:T(8,128)(2,1)S(1)}, bf16[1,1,16,128,128]{4,3,2,1,0:T(8,128)(2,1)}, u32[]{:S(2)}) copy-start(bf16[1,1,16,128,128]{4,3,2,1,0:T(8,128)(2,1)} %param.10) | copy-start | bytes 1572868
  7.2 78.0 %reduce-scatter.3.cloned.1.call-start = ((), (), s32[]{:S(2)}) async-start(), calls=%async_computation.2 | async-start | bytes 786432 | tf_op jit(solution)/shard_map/reduce_scatter | solution.py:61
  76.5 8.7 %copy-start.2 = (bf16[128,512]{1,0:T(8,128)(2,1)S(1)}, bf16[128,512]{1,0:T(8,128)(2,1)}, u32[]{:S(2)}) copy-start(bf16[128,512]{1,0:T(8,128)(2,1)} %param.13) | copy-start | bytes 393220
  76.5 8.7 %copy-start.4 = (f32[512]{0:T(512)S(1)}, f32[512]{0:T(512)}, u32[]{:S(2)}) copy-start(f32[512]{0:T(512)} %param.9) | copy-start | bytes 6148
  81.2 122.8 %reduce-scatter.5.cloned.1.call-start = ((), (), s32[]{:S(2)}) async-start(), calls=%async_computation.3 | async-start | bytes 4456448 | tf_op jit(solution)/shard_map/reduce_scatter | solution.py:81
  106.8 97.3 %copy-start.3 = (bf16[128,128]{1,0:T(8,128)(2,1)S(1)}, bf16[128,128]{1,0:T(8,128)(2,1)}, u32[]{:S(2)}) copy-start(bf16[128,128]{1,0:T(8,128)(2,1)} %param.7) | copy-start | bytes 98308
  106.8 99.3 %copy-start.1 = (bf16[128,512]{1,0:T(8,128)(2,1)S(1)}, bf16[128,512]{1,0:T(8,128)(2,1)}, u32[]{:S(2)}) copy-start(bf16[128,512]{1,0:T(8,128)(2,1)} %param.8) | copy-start | bytes 393220
  106.8 228.8 %all-reduce.2.cloned.1.call-start = ((), (), s32[]{:S(2)}) async-start(), calls=%async_computation.4 | async-start | bytes 524288 | tf_op jit(solution)/shard_map/psum | solution.py:86
Sparse Core Ops, SparseCore 0:
  81.4 3.8 reduce-scatter.2
  106.9 97.0 reduce-scatter.4
  211.0 124.5 all-reduce.1
where the time goes:
time: 345 us; the launch traced here: 344 us
  waiting for transfers between devices  183 us (53%)
  blocking collectives  93.5 us (27%)
  matrix products  26 us (8%)
  local copies, waits for them, and re-layouts  23.7 us (7%)
  between operations  14.5 us (4%)
    psum x1, waiting for transfers between devices, local(): grad_weight = lax.psum(weight_part, ('row', 'col'))  128 us
    reduce_scatter x1, waiting for transfers between devices, local(): dproj = lax.psum_scatter(dproj_part, 'col', scatter_dimension=0, tiled=True)  51.5 us
    psum x1, blocking collectives, local(): grad_bias = lax.psum(bias_part, ('row', 'col'))  45.7 us
    all_gather x1, blocking collectives, local(): source_block = lax.all_gather(features, 'col', axis=0, tiled=True)  45.6 us
    dot_general x2, matrix products, step(): jnp.einsum('tk,kah->tah', onehot, prod, precision=lax.Precision.HIGHEST)  8.07 us
    dot_general x1, matrix products, step(): jnp.einsum('kab,kbh->kah', part_tiles.astype(jnp.float32), picked, precis...  7.66 us
  transfers between devices with their start and end apart: 3, of which 3 were waited for; matrix products, arithmetic and copies ran while one was open for 1% of the time, Pallas kernels for 0%

commit v1 on v0

v1 whole, which is shorter than its diff:
```python
import functools

import jax
import jax.numpy as jnp
from jax import lax
from jax.experimental import pallas as pl
from jax.experimental.pallas import tpu as pltpu
from jax.sharding import PartitionSpec as P

MESH = pl.DeviceIdType.MESH
F32 = jnp.float32
BF16 = jnp.bfloat16
GROUP = 16


def nearest_first(count):
    return sorted(range(1, count), key=lambda d: (min(d, count - d), d))


def remote(src, dst, send, recv, device):
    return pltpu.make_async_remote_copy(
        src_ref=src, dst_ref=dst, send_sem=send, recv_sem=recv, device_id=device, device_id_type=MESH
    )


def kernel(
    n_row, n_col, inner,
    features, weight, bias, tiles_in, index, count, cotangent,
    hidden_out, gf_out, gw_out, gb_out,
    x, w, b, tiles, adj, cot, hpart, hid, dpre,
    ssend, srecv, zsend, zrecv, gsend, grecv, gfull, bparts, gf,
    load_sem, store_sem, x_send, x_recv, c_send, c_recv, h_send, h_recv,
    s_send, s_recv, z_send, z_recv, g_send, g_recv, a_send, a_recv, b_send, b_recv,
):
    r = lax.axis_index("row")
    c = lax.axis_index("col")
    outer = n_col // inner
    hi = c // inner
    lo = lax.rem(c, inner)
    rows = features.shape[0]
    own_rows = cot.shape[1]
    width = w.shape[1]
    slots, size = tiles.shape[0], tiles.shape[1]
    tile_cols = n_col * rows // size
    tile_rows = n_row * own_rows // size

    def block(col):
        return pl.ds(pl.multiple_of(col * rows, rows), rows)

    def col_of(turn_hi, turn_lo):
        return lax.rem(hi + turn_hi, outer) * inner + lax.rem(lo + turn_lo, inner)

    load_x = pltpu.make_async_copy(features, x.at[block(c)], load_sem.at[0])
    load_c = pltpu.make_async_copy(cotangent, cot.at[r], load_sem.at[1])
    load_t = pltpu.make_async_copy(tiles_in.at[0, 0], tiles, load_sem.at[2])
    load_w = pltpu.make_async_copy(weight, w, load_sem.at[3])
    load_b = pltpu.make_async_copy(bias, b, load_sem.at[4])
    for load in (load_x, load_c, load_t, load_w, load_b):
        load.start()

    barrier = pltpu.get_barrier_semaphore()
    for d in range(1, n_col):
        pl.semaphore_signal(barrier, inc=1, device_id=(r, lax.rem(c + d, n_col)), device_id_type=MESH)
    for d in range(1, n_row):
        pl.semaphore_signal(barrier, inc=1, device_id=(lax.rem(r + d, n_row), c), device_id_type=MESH)
    pl.semaphore_wait(barrier, n_col + n_row - 2)

    pending = []

    def send(copy):
        copy.start()
        pending.append(copy)

    def send_x(number, source, to):
        send(remote(x.at[block(source)], x.at[block(source)], x_send.at[number], x_recv.at[source], (r, to)))

    def wait_x(source):
        remote(x.at[block(source)], x.at[block(source)], x_send.at[0], x_recv.at[source], (r, c)).wait_recv()

    number = 0
    load_x.wait()
    for d in nearest_first(outer):
        send_x(number, c, col_of(d, 0))
        number += 1
    for q in range(1, inner):
        send_x(number, c, col_of(0, q))
        number += 1
    load_c.wait()
    for d in range(1, n_row):
        send(remote(cot.at[r], cot.at[r], c_send.at[d], c_recv.at[r], (lax.rem(r + d, n_row), c)))

    load_t.wait()
    live = count[0, 0]

    def place(t, carry):
        def find(s, slot):
            return jnp.where((index[0, 0, s] == t) & (s < live), s, slot)

        slot = lax.fori_loop(0, slots, find, jnp.int32(-1), unroll=min(slots, 16))
        tile = tiles[jnp.maximum(slot, 0)]
        row = pl.ds(pl.multiple_of(t // tile_cols * size, size), size)
        column = pl.ds(pl.multiple_of(lax.rem(t, tile_cols) * size, size), size)
        adj[row, column] = jnp.where(slot >= 0, tile, jnp.zeros_like(tile))
        return carry

    lax.fori_loop(0, tile_rows * tile_cols, place, 0)

    for d in nearest_first(outer):
        source = col_of(d, 0)
        wait_x(source)
        for q in range(1, inner):
            send_x(number, source, col_of(0, q))
            number += 1
    for d in [0] + nearest_first(outer):
        for q in range(1, inner):
            wait_x(col_of(d, q))

    total_rows = n_row * own_rows
    step = min(256, total_rows)
    for at in range(0, total_rows, step):
        hpart[r, at : at + step, :] = jnp.dot(adj[at : at + step, :], x[...], preferred_element_type=F32)
    for d in range(1, n_row):
        send(remote(hpart.at[r], hpart.at[r], h_send.at[d], h_recv.at[r], (lax.rem(r + d, n_row), c)))
    load_w.wait()
    load_b.wait()
    for d in range(1, n_row):
        other = lax.rem(r + d, n_row)
        remote(cot.at[other], cot.at[other], c_send.at[0], c_recv.at[other], (r, c)).wait_recv()
    for d in range(1, n_row):
        other = lax.rem(r + d, n_row)
        remote(hpart.at[other], hpart.at[other], h_send.at[0], h_recv.at[other], (r, c)).wait_recv()
    h = hpart[0]
    for k in range(1, n_row):
        h = h + hpart[k]
    hb = h.astype(BF16)
    ht = h.T.astype(BF16)

    bias_sum = jnp.zeros((1, width), F32)
    for k in range(n_row):
        part = hb[k * own_rows : (k + 1) * own_rows]
        pre = jnp.dot(part, w[...], preferred_element_type=F32) + b[...]
        sig = jax.nn.sigmoid(pre)
        hid[k] = (pre * sig).astype(BF16)
        grad = (cot[k].astype(F32) * (sig + pre * sig * (1.0 - sig))).astype(BF16)
        dpre[k * own_rows : (k + 1) * own_rows, :] = grad
        bias_sum = bias_sum + jnp.sum(grad.astype(F32), axis=0, keepdims=True)
    store_h = pltpu.make_async_copy(hid.at[r], hidden_out, store_sem.at[0])
    store_h.start()

    gt = lax.dot_general(w[...], dpre[...], (((1,), (1,)), ((), ())), preferred_element_type=F32).astype(BF16)
    lanes = inner * rows
    for d in nearest_first(outer) + [0]:
        to = lax.rem(hi + d, outer)
        columns = pl.ds(pl.multiple_of(to * lanes, lanes), lanes)
        part = jnp.dot(gt, adj[:, columns], preferred_element_type=F32).astype(BF16)
        for q in range(inner):
            ssend[d, q] = part[:, q * rows : (q + 1) * rows]
        for q in range(1, inner):
            at = lax.rem(lo + q, inner)
            send(remote(ssend.at[d, at], srecv.at[d, lo], s_send.at[d, q], s_recv.at[d, lo], (r, hi * inner + at)))

    gw = jnp.dot(ht, dpre[...], preferred_element_type=F32).astype(BF16)
    chunk = gsend.shape[2]
    parts = width // chunk
    for k in range(n_col):
        g, l = k // parts, k % parts
        gsend[k] = gw[g * GROUP : (g + 1) * GROUP, l * chunk : (l + 1) * chunk]
    bparts[c] = bias_sum
    grecv[c] = gsend[c]
    for d in range(1, n_col):
        to = lax.rem(c + d, n_col)
        send(remote(gsend.at[to], grecv.at[c], g_send.at[d], g_recv.at[c], (r, to)))
    for d in range(1, n_col):
        to = lax.rem(c + d, n_col)
        send(remote(bparts.at[c], bparts.at[c], b_send.at[d], b_recv.at[c], (r, to)))

    own_sum = None
    for d in nearest_first(outer) + [0]:
        for q in range(1, inner):
            at = lax.rem(lo + q, inner)
            remote(ssend.at[d, at], srecv.at[d, at], s_send.at[0, 0], s_recv.at[d, at], (r, c)).wait_recv()
        part = ssend[d, lo].astype(F32)
        for q in range(1, inner):
            part = part + srecv[d, lax.rem(lo + q, inner)].astype(F32)
        if d:
            to = lax.rem(hi + d, outer)
            zsend[d] = part.astype(BF16)
            send(remote(zsend.at[d], zrecv.at[hi], z_send.at[d], z_recv.at[hi], (r, to * inner + lo)))
        else:
            own_sum = part

    for d in range(1, n_col):
        source = lax.rem(c + d, n_col)
        remote(gsend.at[0], grecv.at[source], g_send.at[0], g_recv.at[source], (r, c)).wait_recv()
    total = grecv[0].astype(F32)
    for k in range(1, n_col):
        total = total + grecv[k].astype(F32)
    gfull[c] = total.astype(BF16)
    for d in range(1, n_col):
        to = lax.rem(c + d, n_col)
        send(remote(gfull.at[c], gfull.at[c], a_send.at[d], a_recv.at[c], (r, to)))

    for d in nearest_first(outer):
        source = lax.rem(hi + d, outer)
        remote(zsend.at[0], zrecv.at[source], z_send.at[0], z_recv.at[source], (r, c)).wait_recv()
        own_sum = own_sum + zrecv[source].astype(F32)
    gf[...] = own_sum.T.astype(BF16)
    store_f = pltpu.make_async_copy(gf, gf_out, store_sem.at[1])
    store_f.start()

    for d in range(1, n_col):
        source = lax.rem(c + d, n_col)
        remote(bparts.at[source], bparts.at[source], b_send.at[0], b_recv.at[source], (r, c)).wait_recv()
    bias_total = bparts[0]
    for k in range(1, n_col):
        bias_total = bias_total + bparts[k]
    gb_out[...] = bias_total
    for d in range(1, n_col):
        source = lax.rem(c + d, n_col)
        remote(gfull.at[source], gfull.at[source], a_send.at[0], a_recv.at[source], (r, c)).wait_recv()
    for k in range(n_col):
        g, l = k // parts, k % parts
        gw_out[g * GROUP : (g + 1) * GROUP, l * chunk : (l + 1) * chunk] = gfull[k].astype(F32)
    for copy in pending:
        copy.wait_send()
    store_h.wait()
    store_f.wait()


def local(n_row, n_col, features, weight, bias, tile_values, tile_index, tile_count, cotangent):
    rows, feat = features.shape
    own_rows, width = cotangent.shape
    slots, size = tile_values.shape[2], tile_values.shape[3]
    inner = 4
    outer = n_col // inner
    target = n_row * own_rows
    source = n_col * rows
    chunk = feat * width // (GROUP * n_col)
    dma = pltpu.SemaphoreType.DMA
    any_spec = pl.BlockSpec(memory_space=pl.ANY)
    smem = pl.BlockSpec(memory_space=pltpu.SMEM)
    vmem = pl.BlockSpec(memory_space=pltpu.VMEM)
    hidden, gf, gw, gb = pl.pallas_call(
        functools.partial(kernel, n_row, n_col, inner),
        out_shape=(
            jax.ShapeDtypeStruct((own_rows, width), BF16),
            jax.ShapeDtypeStruct((rows, feat), BF16),
            jax.ShapeDtypeStruct((feat, width), F32),
            jax.ShapeDtypeStruct((1, width), F32),
        ),
        in_specs=[any_spec, any_spec, any_spec, any_spec, smem, smem, any_spec],
        out_specs=(any_spec, any_spec, vmem, vmem),
        scratch_shapes=[
            pltpu.VMEM((source, feat), BF16),
            pltpu.VMEM((feat, width), BF16),
            pltpu.VMEM((1, width), F32),
            pltpu.VMEM((slots, size, size), BF16),
            pltpu.VMEM((target, source), BF16),
            pltpu.VMEM((n_row, own_rows, width), BF16),
            pltpu.VMEM((n_row, target, feat), F32),
            pltpu.VMEM((n_row, own_rows, width), BF16),
            pltpu.VMEM((target, width), BF16),
            pltpu.VMEM((outer, inner, feat, rows), BF16),
            pltpu.VMEM((outer, inner, feat, rows), BF16),
            pltpu.VMEM((outer, feat, rows), BF16),
            pltpu.VMEM((outer, feat, rows), BF16),
            pltpu.VMEM((n_col, GROUP, chunk), BF16),
            pltpu.VMEM((n_col, GROUP, chunk), BF16),
            pltpu.VMEM((n_col, GROUP, chunk), BF16),
            pltpu.VMEM((n_col, 1, width), F32),
            pltpu.VMEM((rows, feat), BF16),
            dma((5,)), dma((2,)),
            dma((n_col,)), dma((n_col,)),
            dma((n_row,)), dma((n_row,)),
            dma((n_row,)), dma((n_row,)),
            dma((outer, inner)), dma((outer, inner)),
            dma((outer,)), dma((outer,)),
            dma((n_col,)), dma((n_col,)),
            dma((n_col,)), dma((n_col,)),
            dma((n_col,)), dma((n_col,)),
        ],
        compiler_params=pltpu.CompilerParams(
            collective_id=0, has_side_effects=True, vmem_limit_bytes=48 * 1024 * 1024
        ),
        cost_estimate=pl.CostEstimate(
            flops=4 * target * source * feat + 6 * target * width * feat,
            bytes_accessed=2 * (slots * size * size + 3 * own_rows * width),
            transcendentals=target * width,
        ),
    )(features, weight, bias.reshape(1, width), tile_values, tile_index, tile_count, cotangent)
    return hidden, gf, gw, gb.reshape(width)


def solution(mesh):
    in_specs = (
        P(("row", "col"), None),
        P(),
        P(),
        P("row", "col", None, None, None),
        P("row", "col", None),
        P("row", "col"),
        P(("col", "row"), None),
    )
    out_specs = (P(("col", "row"), None), P(("row", "col"), None), P(), P())
    body = functools.partial(local, mesh.shape["row"], mesh.shape["col"])
    return jax.shard_map(body, mesh=mesh, in_specs=in_specs, out_specs=out_specs, check_vma=False)
```

time: 345 us -> 42.5 us (0.12)
  waiting for transfers between devices: 183 us -> 0 us
  blocking collectives: 93.5 us -> 0 us
  Pallas kernels: 0 us -> 34.1 us
  matrix products: 26 us -> 0 us
  local copies, waits for them, and re-layouts: 23.7 us -> 6.8 us
  between operations: 14.5 us -> 1.33 us
    psum x1 -> x0, waiting for transfers between devices: 128 us -> none  [local(): grad_weight = lax.psum(weight_part, ('row', 'col'))]
    reduce_scatter x2 -> x0, waiting for transfers between devices: 55.4 us -> none  [the longest x1 51.5 us: local(): dproj = lax.psum_scatter(dproj_part, 'col', scatter_dimension=0, tiled=True)]
    all_gather x2 -> x0, blocking collectives: 47.7 us -> none  [the longest x1 45.6 us: local(): source_block = lax.all_gather(features, 'col', axis=0, tiled=True)]
    psum x1 -> x0, blocking collectives: 45.7 us -> none  [local(): grad_bias = lax.psum(bias_part, ('row', 'col'))]
    pallas_call x0 -> x1, Pallas kernels: none -> 34.1 us  [local(): pl.pallas_call(functools.partial(kernel, n_row, n_col, inner), out_shape=...]
    dot_general x7 -> x0, matrix products: 26 us -> none  [the longest x2 8.07 us: step(): jnp.einsum('tk,kah->tah', onehot, prod, precision=lax.Precision.HIGHEST)]
    dot_general x4 -> x0, local copies, waits for them, and re-layouts: 16.3 us -> none  [the longest x1 5.53 us: step(): jnp.einsum('kab,kbh->kah', part_tiles.astype(jnp.float32), picked, precis...]
    gather x2 -> x0, local copies, waits for them, and re-layouts: 5.61 us -> none  [step(): picked = jnp.take(source, part_take, axis=0)]
  transfers between devices with their start and end apart: 3 -> 0, of which waited for: 3 -> 0; matrix products, arithmetic and copies ran while one was open for 1% -> 0% of each run, Pallas kernels for 0% -> 0%
where the time goes in v1:
time: 42.5 us; the launch traced here: 42.2 us
  Pallas kernels  34.1 us (80%)
  local copies, waits for them, and re-layouts  6.8 us (16%)
  between operations  1.33 us (3%)
    pallas_call x1, Pallas kernels, local(): pl.pallas_call(functools.partial(kernel, n_row, n_col, inner), out_shape=...  34.1 us
    unnamed x16, local copies, waits for them, and re-layouts  6.8 us

profile of v1, /device:TPU:0, one launch (start us, length us, event | category | flops | bytes accessed | tf_op | source)
XLA Modules:
  0.0 42.2 jit_solution(3088645309923114783)
XLA Ops:
  0.6 0.0 copy-start.4
  1.3 0.0 copy-start.5
  1.3 0.0 copy-done.4
  1.3 0.6 %copy-done.5 = s32[1,1,16]{2,1,0:T(1,128)S(1)} copy-done((s32[1,1,16]{2,1,0:T(1,128)S(1)}, s32[1,1,16]{2,1,0:T(1,128)}, u32[]{:S(2)}) %copy-start.5) | copy-done | bytes 88
  2.0 0.0 copy-start
  2.0 1.0 %copy-done = bf16[1,1,16,128,128]{4,3,2,1,0:T(8,128)(2,1)S(1)} copy-done((bf16[1,1,16,128,128]{4,3,2,1,0:T(8,128)(2,1)S(1)}, bf16[1,1,16,128,128]{4,3,2,1,0:T(8,128)(2,1)}, u32[]{:S(2)}) %copy-start) | copy-done | bytes 524312
  3.0 0.0 copy-start.1
  3.0 0.9 %copy-done.1 = bf16[128,512]{1,0:T(8,128)(2,1)S(1)} copy-done((bf16[128,512]{1,0:T(8,128)(2,1)S(1)}, bf16[128,512]{1,0:T(8,128)(2,1)}, u32[]{:S(2)}) %copy-start.1) | copy-done | bytes 131096
  3.9 0.0 copy-start.2
  3.9 0.9 %copy-done.2 = bf16[128,512]{1,0:T(8,128)(2,1)S(1)} copy-done((bf16[128,512]{1,0:T(8,128)(2,1)S(1)}, bf16[128,512]{1,0:T(8,128)(2,1)}, u32[]{:S(2)}) %copy-start.2) | copy-done | bytes 131096
  4.8 0.0 copy-start.3
  4.8 0.8 %copy-done.3 = bf16[128,128]{1,0:T(8,128)(2,1)S(1)} copy-done((bf16[128,128]{1,0:T(8,128)(2,1)S(1)}, bf16[128,128]{1,0:T(8,128)(2,1)}, u32[]{:S(2)}) %copy-start.3) | copy-done | bytes 32792
  5.6 34.1 %shard_map.102 = (bf16[128,512]{1,0:T(8,128)(2,1)S(1)}, bf16[128,128]{1,0:T(8,128)(2,1)S(1)}, f32[128,512]{1,0:T(8,128)S(1)}, f32[1,512]{1,0:T(1,128)S(1)}) custom-call(bf16[128,128]{1,0:T(8,128)(2,1)S(1)} %copy-done.3, bf16[128,512]{1,0:T(8,128)(2,1)S(1)} %copy-done.1, f32[1,512]{1,0:T(1,128)S(1)} %bitcast.3, bf16[1,1,16,128,128]{4,3,2,1,0:T(8,128)(2,1)S(1)} %copy-done, ...), custom_call_target="tpu_custom_call" | custom-call | flops 369098752 | bytes 917504 | tf_op jit(solution)/shard_map/pallas_call | solution.py:243
  39.6 0.7 %copy.16 = bf16[128,512]{1,0:T(8,128)(2,1)} copy(bf16[128,512]{1,0:T(8,128)(2,1)S(1)} %get-tuple-element.16) | data formatting | bytes 262144
  40.3 0.6 %copy.17 = bf16[128,128]{1,0:T(8,128)(2,1)} copy(bf16[128,128]{1,0:T(8,128)(2,1)S(1)} %get-tuple-element.17) | data formatting | bytes 65536
  40.9 0.7 %copy.18 = f32[128,512]{1,0:T(8,128)} copy(f32[128,512]{1,0:T(8,128)S(1)} %get-tuple-element.18) | data formatting | bytes 524288
  41.6 0.6 %copy.19 = f32[512]{0:T(512)} copy(f32[512]{0:T(512)S(1)} %bitcast.2) | data formatting | bytes 4096
Async XLA Ops:
  0.6 0.7 %copy-start.4 = (f32[512]{0:T(512)S(1)}, f32[512]{0:T(512)}, u32[]{:S(2)}) copy-start(f32[512]{0:T(512)} %param.9) | copy-start | bytes 6148
  1.3 0.7 %copy-start.5 = (s32[1,1,16]{2,1,0:T(1,128)S(1)}, s32[1,1,16]{2,1,0:T(1,128)}, u32[]{:S(2)}) copy-start(s32[1,1,16]{2,1,0:T(1,128)} %index.1) | copy-start | bytes 196
  2.0 1.0 %copy-start = (bf16[1,1,16,128,128]{4,3,2,1,0:T(8,128)(2,1)S(1)}, bf16[1,1,16,128,128]{4,3,2,1,0:T(8,128)(2,1)}, u32[]{:S(2)}) copy-start(bf16[1,1,16,128,128]{4,3,2,1,0:T(8,128)(2,1)} %tiles_in.1) | copy-start | bytes 1572868
  3.0 0.9 %copy-start.1 = (bf16[128,512]{1,0:T(8,128)(2,1)S(1)}, bf16[128,512]{1,0:T(8,128)(2,1)}, u32[]{:S(2)}) copy-start(bf16[128,512]{1,0:T(8,128)(2,1)} %weight.1) | copy-start | bytes 393220
  3.9 0.9 %copy-start.2 = (bf16[128,512]{1,0:T(8,128)(2,1)S(1)}, bf16[128,512]{1,0:T(8,128)(2,1)}, u32[]{:S(2)}) copy-start(bf16[128,512]{1,0:T(8,128)(2,1)} %cotangent.1) | copy-start | bytes 393220
  4.8 0.8 %copy-start.3 = (bf16[128,128]{1,0:T(8,128)(2,1)S(1)}, bf16[128,128]{1,0:T(8,128)(2,1)}, u32[]{:S(2)}) copy-start(bf16[128,128]{1,0:T(8,128)(2,1)} %features.1) | copy-start | bytes 98308

commit v2 on v1

--- a/solution.py
+++ b/solution.py
@@ -24,19 +24,31 @@
 
 
 def kernel(
-    n_row, n_col, inner,
-    features, weight, bias, tiles_in, index, count, cotangent,
+    n_row, n_col, inner, split,
+    features, weight, bias, tiles_in, index_in, count, cotangent,
     hidden_out, gf_out, gw_out, gb_out,
-    x, w, b, tiles, adj, cot, hpart, hid, dpre,
-    ssend, srecv, zsend, zrecv, gsend, grecv, gfull, bparts, gf,
+    x, w, b, tiles, adj, cot, hpart, hts, hid, dpre,
+    ssend, srecv, zsend, zrecv, gsend, grecv, gfull, bparts, gf, index,
     load_sem, store_sem, x_send, x_recv, c_send, c_recv, h_send, h_recv,
-    s_send, s_recv, z_send, z_recv, g_send, g_recv, a_send, a_recv, b_send, b_recv,
+    s_send, s_recv, z_send, z_recv, g_send, g_recv, a_send, a_recv, b_send, b_recv, p_send, p_recv,
 ):
     r = lax.axis_index("row")
     c = lax.axis_index("col")
     outer = n_col // inner
     hi = c // inner
     lo = lax.rem(c, inner)
+    swap = lax.rem(r, 2) if outer == inner else 0
+    a = hi + swap * (lo - hi)
+    b_at = lo + swap * (hi - lo)
+
+    def col_at(first, second):
+        return (first + swap * (second - first)) * inner + second + swap * (first - second)
+
+    def place_of(col):
+        high, low = col // inner, lax.rem(col, inner)
+        return (high + swap * (low - high)) * inner + low + swap * (high - low)
+
+    me = a * inner + b_at
     rows = features.shape[0]
     own_rows = cot.shape[1]
     width = w.shape[1]
@@ -44,18 +56,26 @@
     tile_cols = n_col * rows // size
     tile_rows = n_row * own_rows // size
 
-    def block(col):
-        return pl.ds(pl.multiple_of(col * rows, rows), rows)
-
-    def col_of(turn_hi, turn_lo):
-        return lax.rem(hi + turn_hi, outer) * inner + lax.rem(lo + turn_lo, inner)
-
-    load_x = pltpu.make_async_copy(features, x.at[block(c)], load_sem.at[0])
+    def block(spot):
+        return pl.ds(pl.multiple_of(spot * rows, rows), rows)
+
+    def turned(turn_a, turn_b):
+        return lax.rem(a + turn_a, outer), lax.rem(b_at + turn_b, inner)
+
+    def spot_of(turn_a, turn_b):
+        first, second = turned(turn_a, turn_b)
+        return first * inner + second
+
+    def col_of(turn_a, turn_b):
+        return col_at(*turned(turn_a, turn_b))
+
+    load_x = pltpu.make_async_copy(features, x.at[block(me)], load_sem.at[0])
     load_c = pltpu.make_async_copy(cotangent, cot.at[r], load_sem.at[1])
     load_t = pltpu.make_async_copy(tiles_in.at[0, 0], tiles, load_sem.at[2])
     load_w = pltpu.make_async_copy(weight, w, load_sem.at[3])
     load_b = pltpu.make_async_copy(bias, b, load_sem.at[4])
-    for load in (load_x, load_c, load_t, load_w, load_b):
+    load_i = pltpu.make_async_copy(index_in, index, load_sem.at[5])
+    for load in (load_x, load_c, load_t, load_w, load_b, load_i):
         load.start()
 
     barrier = pltpu.get_barrier_semaphore()
@@ -80,16 +100,17 @@
     number = 0
     load_x.wait()
     for d in nearest_first(outer):
-        send_x(number, c, col_of(d, 0))
+        send_x(number, me, col_of(d, 0))
         number += 1
     for q in range(1, inner):
-        send_x(number, c, col_of(0, q))
+        send_x(number, me, col_of(0, q))
         number += 1
     load_c.wait()
     for d in range(1, n_row):
         send(remote(cot.at[r], cot.at[r], c_send.at[d], c_recv.at[r], (lax.rem(r + d, n_row), c)))
 
     load_t.wait()
+    load_i.wait()
     live = count[0, 0]
 
     def place(t, carry):
@@ -99,21 +120,21 @@
         slot = lax.fori_loop(0, slots, find, jnp.int32(-1), unroll=min(slots, 16))
         tile = tiles[jnp.maximum(slot, 0)]
         row = pl.ds(pl.multiple_of(t // tile_cols * size, size), size)
-        column = pl.ds(pl.multiple_of(lax.rem(t, tile_cols) * size, size), size)
+        column = pl.ds(pl.multiple_of(place_of(lax.rem(t, tile_cols)) * size, size), size)
         adj[row, column] = jnp.where(slot >= 0, tile, jnp.zeros_like(tile))
         return carry
 
     lax.fori_loop(0, tile_rows * tile_cols, place, 0)
 
     for d in nearest_first(outer):
-        source = col_of(d, 0)
+        source = spot_of(d, 0)
         wait_x(source)
         for q in range(1, inner):
             send_x(number, source, col_of(0, q))
             number += 1
     for d in [0] + nearest_first(outer):
         for q in range(1, inner):
-            wait_x(col_of(d, q))
+            wait_x(spot_of(d, q))
 
     total_rows = n_row * own_rows
     step = min(256, total_rows)
@@ -133,7 +154,7 @@
     for k in range(1, n_row):
         h = h + hpart[k]
     hb = h.astype(BF16)
-    ht = h.T.astype(BF16)
+    hts[...] = h.T.astype(BF16)
 
     bias_sum = jnp.zeros((1, width), F32)
     for k in range(n_row):
@@ -147,19 +168,9 @@
     store_h = pltpu.make_async_copy(hid.at[r], hidden_out, store_sem.at[0])
     store_h.start()
 
-    gt = lax.dot_general(w[...], dpre[...], (((1,), (1,)), ((), ())), preferred_element_type=F32).astype(BF16)
-    lanes = inner * rows
-    for d in nearest_first(outer) + [0]:
-        to = lax.rem(hi + d, outer)
-        columns = pl.ds(pl.multiple_of(to * lanes, lanes), lanes)
-        part = jnp.dot(gt, adj[:, columns], preferred_element_type=F32).astype(BF16)
-        for q in range(inner):
-            ssend[d, q] = part[:, q * rows : (q + 1) * rows]
-        for q in range(1, inner):
-            at = lax.rem(lo + q, inner)
-            send(remote(ssend.at[d, at], srecv.at[d, lo], s_send.at[d, q], s_recv.at[d, lo], (r, hi * inner + at)))
-
-    gw = jnp.dot(ht, dpre[...], preferred_element_type=F32).astype(BF16)
+    half = lax.rem(r, split)
+    deep = hts.shape[0] // split
+    gw = jnp.dot(hts[pl.ds(pl.multiple_of(half * deep, deep), deep), :], dpre[...], preferred_element_type=F32).astype(BF16)
     chunk = gsend.shape[2]
     parts = width // chunk
     for k in range(n_col):
@@ -170,24 +181,22 @@
     for d in range(1, n_col):
         to = lax.rem(c + d, n_col)
         send(remote(gsend.at[to], grecv.at[c], g_send.at[d], g_recv.at[c], (r, to)))
+
+    gt = lax.dot_general(w[...], dpre[...], (((1,), (1,)), ((), ())), preferred_element_type=F32).astype(BF16)
+    lanes = inner * rows
+    for d in nearest_first(outer) + [0]:
+        to = lax.rem(a + d, outer)
+        columns = pl.ds(pl.multiple_of(to * lanes, lanes), lanes)
+        part = jnp.dot(gt, adj[:, columns], preferred_element_type=F32).astype(BF16)
+        for q in range(inner):
+            ssend[d, q] = part[:, q * rows : (q + 1) * rows]
+        for q in range(1, inner):
+            at = lax.rem(b_at + q, inner)
+            send(remote(ssend.at[d, at], srecv.at[d, b_at], s_send.at[d, q], s_recv.at[d, b_at], (r, col_at(a, at))))
+
     for d in range(1, n_col):
         to = lax.rem(c + d, n_col)
         send(remote(bparts.at[c], bparts.at[c], b_send.at[d], b_recv.at[c], (r, to)))
-
-    own_sum = None
-    for d in nearest_first(outer) + [0]:
-        for q in range(1, inner):
-            at = lax.rem(lo + q, inner)
-            remote(ssend.at[d, at], srecv.at[d, at], s_send.at[0, 0], s_recv.at[d, at], (r, c)).wait_recv()
-        part = ssend[d, lo].astype(F32)
-        for q in range(1, inner):
-            part = part + srecv[d, lax.rem(lo + q, inner)].astype(F32)
-        if d:
-            to = lax.rem(hi + d, outer)
-            zsend[d] = part.astype(BF16)
-            send(remote(zsend.at[d], zrecv.at[hi], z_send.at[d], z_recv.at[hi], (r, to * inner + lo)))
-        else:
-            own_sum = part
 
     for d in range(1, n_col):
         source = lax.rem(c + d, n_col)
@@ -195,13 +204,34 @@
     total = grecv[0].astype(F32)
     for k in range(1, n_col):
         total = total + grecv[k].astype(F32)
-    gfull[c] = total.astype(BF16)
+    gfull[half, c] = total.astype(BF16)
     for d in range(1, n_col):
         to = lax.rem(c + d, n_col)
-        send(remote(gfull.at[c], gfull.at[c], a_send.at[d], a_recv.at[c], (r, to)))
-
+        send(remote(gfull.at[half, c], gfull.at[half, c], a_send.at[d], a_recv.at[c], (r, to)))
+
+    own_sum = None
+    for d in nearest_first(outer) + [0]:
+        for q in range(1, inner):
+            at = lax.rem(b_at + q, inner)
+            remote(ssend.at[d, at], srecv.at[d, at], s_send.at[0, 0], s_recv.at[d, at], (r, c)).wait_recv()
+        part = ssend[d, b_at].astype(F32)
+        for q in range(1, inner):
+            part = part + srecv[d, lax.rem(b_at + q, inner)].astype(F32)
+        if d:
+            to = lax.rem(a + d, outer)
+            zsend[d] = part.astype(BF16)
+            send(remote(zsend.at[d], zrecv.at[a], z_send.at[d], z_recv.at[a], (r, col_at(to, b_at))))
+        else:
+            own_sum = part
+
+    for d in range(1, n_col):
+        source = lax.rem(c + d, n_col)
+        remote(gfull.at[half, source], gfull.at[half, source], a_send.at[0], a_recv.at[source], (r, c)).wait_recv()
+    if split == 2:
+        partner = r + 1 - 2 * half
+        send(remote(gfull.at[half], gfull.at[half], p_send.at[0], p_recv.at[0], (partner, c)))
     for d in nearest_first(outer):
-        source = lax.rem(hi + d, outer)
+        source = lax.rem(a + d, outer)
         remote(zsend.at[0], zrecv.at[source], z_send.at[0], z_recv.at[source], (r, c)).wait_recv()
         own_sum = own_sum + zrecv[source].astype(F32)
     gf[...] = own_sum.T.astype(BF16)
@@ -215,16 +245,25 @@
     for k in range(1, n_col):
         bias_total = bias_total + bparts[k]
     gb_out[...] = bias_total
-    for d in range(1, n_col):
-        source = lax.rem(c + d, n_col)
-        remote(gfull.at[source], gfull.at[source], a_send.at[0], a_recv.at[source], (r, c)).wait_recv()
-    for k in range(n_col):
-        g, l = k // parts, k % parts
-        gw_out[g * GROUP : (g + 1) * GROUP, l * chunk : (l + 1) * chunk] = gfull[k].astype(F32)
+    if split == 2:
+        remote(gfull.at[1 - half], gfull.at[1 - half], p_send.at[0], p_recv.at[0], (r, c)).wait_recv()
+    for n in range(split):
+        for k in range(n_col):
+            top, l = n * deep + k // parts * GROUP, k % parts
+            gw_out[top : top + GROUP, l * chunk : (l + 1) * chunk] = gfull[n, k].astype(F32)
     for copy in pending:
         copy.wait_send()
     store_h.wait()
     store_f.wait()
+
+
+def hand_over(*refs):
+    sources, results, sems = refs[:4], refs[4:8], refs[8]
+    copies = [pltpu.make_async_copy(sources[k], results[k], sems.at[k]) for k in range(4)]
+    for copy in copies:
+        copy.start()
+    for copy in copies:
+        copy.wait()
 
 
 def local(n_row, n_col, features, weight, bias, tile_values, tile_index, tile_count, cotangent):
@@ -236,19 +275,21 @@
     target = n_row * own_rows
     source = n_col * rows
     chunk = feat * width // (GROUP * n_col)
+    split = 2 if n_row % 2 == 0 and chunk % 256 == 0 else 1
+    chunk = chunk // split
     dma = pltpu.SemaphoreType.DMA
     any_spec = pl.BlockSpec(memory_space=pl.ANY)
-    smem = pl.BlockSpec(memory_space=pltpu.SMEM)
+    hbm = pl.BlockSpec(memory_space=pltpu.HBM)
     vmem = pl.BlockSpec(memory_space=pltpu.VMEM)
     hidden, gf, gw, gb = pl.pallas_call(
-        functools.partial(kernel, n_row, n_col, inner),
+        functools.partial(kernel, n_row, n_col, inner, split),
         out_shape=(
             jax.ShapeDtypeStruct((own_rows, width), BF16),
             jax.ShapeDtypeStruct((rows, feat), BF16),
             jax.ShapeDtypeStruct((feat, width), F32),
             jax.ShapeDtypeStruct((1, width), F32),
         ),
-        in_specs=[any_spec, any_spec, any_spec, any_spec, smem, smem, any_spec],
+        in_specs=[hbm] * 5 + [pl.BlockSpec(memory_space=pltpu.SMEM), hbm],
         out_specs=(any_spec, any_spec, vmem, vmem),
         scratch_shapes=[
             pltpu.VMEM((source, feat), BF16),
@@ -258,6 +299,7 @@
             pltpu.VMEM((target, source), BF16),
             pltpu.VMEM((n_row, own_rows, width), BF16),
             pltpu.VMEM((n_row, target, feat), F32),
+            pltpu.VMEM((feat, target), BF16),
             pltpu.VMEM((n_row, own_rows, width), BF16),
             pltpu.VMEM((target, width), BF16),
             pltpu.VMEM((outer, inner, feat, rows), BF16),
@@ -266,10 +308,11 @@
             pltpu.VMEM((outer, feat, rows), BF16),
             pltpu.VMEM((n_col, GROUP, chunk), BF16),
             pltpu.VMEM((n_col, GROUP, chunk), BF16),
-            pltpu.VMEM((n_col, GROUP, chunk), BF16),
+            pltpu.VMEM((split, n_col, GROUP, chunk), BF16),
             pltpu.VMEM((n_col, 1, width), F32),
             pltpu.VMEM((rows, feat), BF16),
-            dma((5,)), dma((2,)),
+            pltpu.SMEM(tile_index.shape, jnp.int32),
+            dma((6,)), dma((2,)),
             dma((n_col,)), dma((n_col,)),
             dma((n_row,)), dma((n_row,)),
             dma((n_row,)), dma((n_row,)),
@@ -278,9 +321,10 @@
             dma((n_col,)), dma((n_col,)),
             dma((n_col,)), dma((n_col,)),
             dma((n_col,)), dma((n_col,)),
+            dma((1,)), dma((1,)),
         ],
         compiler_params=pltpu.CompilerParams(
-            collective_id=0, has_side_effects=True, vmem_limit_bytes=48 * 1024 * 1024
+            collective_id=0, has_side_effects=True, vmem_limit_bytes=60 * 1024 * 1024
         ),
         cost_estimate=pl.CostEstimate(
             flops=4 * target * source * feat + 6 * target * width * feat,
@@ -288,6 +332,15 @@
             transcendentals=target * width,
         ),
     )(features, weight, bias.reshape(1, width), tile_values, tile_index, tile_count, cotangent)
+    results = (hidden, gf, gw, gb)
+    hidden, gf, gw, gb = pl.pallas_call(
+        hand_over,
+        out_shape=tuple(jax.ShapeDtypeStruct(value.shape, value.dtype) for value in results),
+        in_specs=[any_spec] * 4,
+        out_specs=(any_spec,) * 4,
+        scratch_shapes=[dma((4,))],
+        compiler_params=pltpu.CompilerParams(vmem_limit_bytes=60 * 1024 * 1024),
+    )(*results)
     return hidden, gf, gw, gb.reshape(width)
 
 

time: 42.5 us -> 48.8 us (1.15)
  Pallas kernels: 34.1 us -> 47.3 us
  local copies, waits for them, and re-layouts: 6.8 us -> 0 us
    pallas_call x1 -> x2, Pallas kernels: 34.1 us -> 47.3 us  [the longest x1 33.2 us: local(): pl.pallas_call(functools.partial(kernel, n_row, n_col, inner, split), out...]
    unnamed x16 -> x0, local copies, waits for them, and re-layouts: 6.8 us -> none
where the time goes in v2:
time: 48.8 us; the launch traced here: 48.6 us
  Pallas kernels  47.3 us (97%)
  between operations  1.29 us (3%)
    pallas_call x1, Pallas kernels, local(): pl.pallas_call(functools.partial(kernel, n_row, n_col, inner, split), out...  33.2 us
    pallas_call x1, Pallas kernels, local(): pl.pallas_call(hand_over, out_shape=tuple((jax.ShapeDtypeStruct(value.sha...  14.1 us

profile of v2, /device:TPU:0, one launch (start us, length us, event | category | flops | bytes accessed | tf_op | source)
XLA Modules:
  0.0 48.6 jit_solution(15635797938140713984)
XLA Ops:
  1.3 33.2 %shard_map.102 = (bf16[128,512]{1,0:T(8,128)(2,1)}, bf16[128,128]{1,0:T(8,128)(2,1)}, f32[128,512]{1,0:T(8,128)}, f32[1,512]{1,0:T(1,128)}) custom-call(bf16[128,128]{1,0:T(8,128)(2,1)} %features.1, bf16[128,512]{1,0:T(8,128)(2,1)} %weight.1, f32[1,512]{1,0:T(1,128)} %bitcast.2, bf16[1,1,16,128,128]{4,3,2,1,0:T(8,128)(2,1)} %tiles_in.1, ...), custom_call_target="tpu_custom_call" | custom-call | flops 369098752 | bytes 917504 | tf_op jit(solution)/shard_map/pallas_call | solution.py:284
  34.5 14.1 %shard_map.103 = (bf16[128,512]{1,0:T(8,128)(2,1)}, bf16[128,128]{1,0:T(8,128)(2,1)}, f32[128,512]{1,0:T(8,128)}, f32[1,512]{1,0:T(1,128)}) custom-call(bf16[128,512]{1,0:T(8,128)(2,1)} %get-tuple-element.12.refs_0_, bf16[128,128]{1,0:T(8,128)(2,1)} %get-tuple-element.13.refs_1_, f32[128,512]{1,0:T(8,128)} %get-tuple-element.14.refs_2_, ...), custom_call_target="tpu_custom_call" | custom-call | tf_op jit(solution)/shard_map/pallas_call | solution.py:336

commit v3 on v2

--- a/solution.py
+++ b/solution.py
@@ -28,9 +28,9 @@
     features, weight, bias, tiles_in, index_in, count, cotangent,
     hidden_out, gf_out, gw_out, gb_out,
     x, w, b, tiles, adj, cot, hpart, hts, hid, dpre,
-    ssend, srecv, zsend, zrecv, gsend, grecv, gfull, bparts, gf, index,
+    ssend, srecv, zsend, zrecv, gsend, grecv, gfull, bparts, bouter, gb, gf, index,
     load_sem, store_sem, x_send, x_recv, c_send, c_recv, h_send, h_recv,
-    s_send, s_recv, z_send, z_recv, g_send, g_recv, a_send, a_recv, b_send, b_recv, p_send, p_recv,
+    s_send, s_recv, z_send, z_recv, g_send, g_recv, a_send, a_recv, b_send, b_recv, p_send, p_recv, d_send, d_recv,
 ):
     r = lax.axis_index("row")
     c = lax.axis_index("col")
@@ -90,6 +90,11 @@
     def send(copy):
         copy.start()
         pending.append(copy)
+
+    def sent():
+        for copy in pending:
+            copy.wait_send()
+        pending.clear()
 
     def send_x(number, source, to):
         send(remote(x.at[block(source)], x.at[block(source)], x_send.at[number], x_recv.at[source], (r, to)))
@@ -132,14 +137,15 @@
         for q in range(1, inner):
             send_x(number, source, col_of(0, q))
             number += 1
+    span = inner * rows
+    partial = None
     for d in [0] + nearest_first(outer):
         for q in range(1, inner):
             wait_x(spot_of(d, q))
-
-    total_rows = n_row * own_rows
-    step = min(256, total_rows)
-    for at in range(0, total_rows, step):
-        hpart[r, at : at + step, :] = jnp.dot(adj[at : at + step, :], x[...], preferred_element_type=F32)
+        group = pl.ds(pl.multiple_of(lax.rem(a + d, outer) * span, span), span)
+        part = jnp.dot(adj[:, group], x[group, :], preferred_element_type=F32)
+        partial = part if partial is None else partial + part
+    hpart[r] = partial
     for d in range(1, n_row):
         send(remote(hpart.at[r], hpart.at[r], h_send.at[d], h_recv.at[r], (lax.rem(r + d, n_row), c)))
     load_w.wait()
@@ -160,7 +166,7 @@
     for k in range(n_row):
         part = hb[k * own_rows : (k + 1) * own_rows]
         pre = jnp.dot(part, w[...], preferred_element_type=F32) + b[...]
-        sig = jax.nn.sigmoid(pre)
+        sig = 0.5 * jnp.tanh(0.5 * pre) + 0.5
         hid[k] = (pre * sig).astype(BF16)
         grad = (cot[k].astype(F32) * (sig + pre * sig * (1.0 - sig))).astype(BF16)
         dpre[k * own_rows : (k + 1) * own_rows, :] = grad
@@ -176,27 +182,28 @@
     for k in range(n_col):
         g, l = k // parts, k % parts
         gsend[k] = gw[g * GROUP : (g + 1) * GROUP, l * chunk : (l + 1) * chunk]
-    bparts[c] = bias_sum
     grecv[c] = gsend[c]
     for d in range(1, n_col):
         to = lax.rem(c + d, n_col)
         send(remote(gsend.at[to], grecv.at[c], g_send.at[d], g_recv.at[c], (r, to)))
 
     gt = lax.dot_general(w[...], dpre[...], (((1,), (1,)), ((), ())), preferred_element_type=F32).astype(BF16)
-    lanes = inner * rows
-    for d in nearest_first(outer) + [0]:
-        to = lax.rem(a + d, outer)
-        columns = pl.ds(pl.multiple_of(to * lanes, lanes), lanes)
+    order = nearest_first(outer) + [0]
+    portion = max(1, outer // 2)
+    for n, d in enumerate(order):
+        columns = pl.ds(pl.multiple_of(lax.rem(a + d, outer) * span, span), span)
         part = jnp.dot(gt, adj[:, columns], preferred_element_type=F32).astype(BF16)
         for q in range(inner):
-            ssend[d, q] = part[:, q * rows : (q + 1) * rows]
-        for q in range(1, inner):
-            at = lax.rem(b_at + q, inner)
-            send(remote(ssend.at[d, at], srecv.at[d, b_at], s_send.at[d, q], s_recv.at[d, b_at], (r, col_at(a, at))))
-
-    for d in range(1, n_col):
-        to = lax.rem(c + d, n_col)
-        send(remote(bparts.at[c], bparts.at[c], b_send.at[d], b_recv.at[c], (r, to)))
+            ssend[q, n] = part[:, q * rows : (q + 1) * rows]
+        if (n + 1) % portion == 0:
+            run, m = pl.ds(n + 1 - portion, portion), n // portion
+            for q in range(1, inner):
+                at = lax.rem(b_at + q, inner)
+                send(remote(ssend.at[at, run], srecv.at[b_at, run], s_send.at[m, q], s_recv.at[m, b_at], (r, col_at(a, at))))
+    bparts[lo] = bias_sum
+    for q in range(1, inner):
+        at = lax.rem(lo + q, inner)
+        send(remote(bparts.at[lo], bparts.at[lo], b_send.at[q], b_recv.at[lo], (r, hi * inner + at)))
 
     for d in range(1, n_col):
         source = lax.rem(c + d, n_col)
@@ -209,60 +216,92 @@
         to = lax.rem(c + d, n_col)
         send(remote(gfull.at[half, c], gfull.at[half, c], a_send.at[d], a_recv.at[c], (r, to)))
 
+    for q in range(1, inner):
+        at = lax.rem(lo + q, inner)
+        remote(bparts.at[at], bparts.at[at], b_send.at[0], b_recv.at[at], (r, c)).wait_recv()
+    bias_sum = bparts[0]
+    for q in range(1, inner):
+        bias_sum = bias_sum + bparts[q]
+    bouter[hi] = bias_sum
+    for d in range(1, outer):
+        to = lax.rem(hi + d, outer)
+        send(remote(bouter.at[hi], bouter.at[hi], d_send.at[d], d_recv.at[hi], (r, to * inner + lo)))
     own_sum = None
-    for d in nearest_first(outer) + [0]:
+    for n, d in enumerate(order):
+        if n % portion == 0:
+            run, m = pl.ds(n, portion), n // portion
+            for q in range(1, inner):
+                at = lax.rem(b_at + q, inner)
+                remote(ssend.at[at, run], srecv.at[at, run], s_send.at[0, 0], s_recv.at[m, at], (r, c)).wait_recv()
+        part = ssend[b_at, n].astype(F32)
         for q in range(1, inner):
-            at = lax.rem(b_at + q, inner)
-            remote(ssend.at[d, at], srecv.at[d, at], s_send.at[0, 0], s_recv.at[d, at], (r, c)).wait_recv()
-        part = ssend[d, b_at].astype(F32)
-        for q in range(1, inner):
-            part = part + srecv[d, lax.rem(b_at + q, inner)].astype(F32)
+            part = part + srecv[lax.rem(b_at + q, inner), n].astype(F32)
         if d:
             to = lax.rem(a + d, outer)
             zsend[d] = part.astype(BF16)
             send(remote(zsend.at[d], zrecv.at[a], z_send.at[d], z_recv.at[a], (r, col_at(to, b_at))))
         else:
             own_sum = part
-
+    sent()
+    for d in range(1, outer):
+        source = lax.rem(hi + d, outer)
+        remote(bouter.at[source], bouter.at[source], d_send.at[0], d_recv.at[source], (r, c)).wait_recv()
+    bias_sum = bouter[0]
+    for k in range(1, outer):
+        bias_sum = bias_sum + bouter[k]
+    gb[...] = bias_sum
+    stores = [store_h]
+
+    def store(source, target, sem):
+        copy = pltpu.make_async_copy(source, target, store_sem.at[sem])
+        copy.start()
+        stores.append(copy)
+
+    store(gb, gb_out, 1)
     for d in range(1, n_col):
         source = lax.rem(c + d, n_col)
         remote(gfull.at[half, source], gfull.at[half, source], a_send.at[0], a_recv.at[source], (r, c)).wait_recv()
     if split == 2:
         partner = r + 1 - 2 * half
         send(remote(gfull.at[half], gfull.at[half], p_send.at[0], p_recv.at[0], (partner, c)))
+    store(gfull.at[half], gw_out.at[half], 2)
     for d in nearest_first(outer):
         source = lax.rem(a + d, outer)
         remote(zsend.at[0], zrecv.at[source], z_send.at[0], z_recv.at[source], (r, c)).wait_recv()
         own_sum = own_sum + zrecv[source].astype(F32)
     gf[...] = own_sum.T.astype(BF16)
-    store_f = pltpu.make_async_copy(gf, gf_out, store_sem.at[1])
-    store_f.start()
-
-    for d in range(1, n_col):
-        source = lax.rem(c + d, n_col)
-        remote(bparts.at[source], bparts.at[source], b_send.at[0], b_recv.at[source], (r, c)).wait_recv()
-    bias_total = bparts[0]
-    for k in range(1, n_col):
-        bias_total = bias_total + bparts[k]
-    gb_out[...] = bias_total
+    store(gf, gf_out, 3)
     if split == 2:
         remote(gfull.at[1 - half], gfull.at[1 - half], p_send.at[0], p_recv.at[0], (r, c)).wait_recv()
-    for n in range(split):
-        for k in range(n_col):
-            top, l = n * deep + k // parts * GROUP, k % parts
-            gw_out[top : top + GROUP, l * chunk : (l + 1) * chunk] = gfull[n, k].astype(F32)
-    for copy in pending:
-        copy.wait_send()
-    store_h.wait()
-    store_f.wait()
-
-
-def hand_over(*refs):
-    sources, results, sems = refs[:4], refs[4:8], refs[8]
-    copies = [pltpu.make_async_copy(sources[k], results[k], sems.at[k]) for k in range(4)]
-    for copy in copies:
-        copy.start()
-    for copy in copies:
+        store(gfull.at[1 - half], gw_out.at[1 - half], 4)
+    sent()
+    for copy in stores:
+        copy.wait()
+
+
+def hand_over(hidden_in, gf_in, gw_in, gb_in, hidden_out, gf_out, gw_out, gb_out, hidden, gf, gw, wide, gb, load_sem, store_sem):
+    chunk = gw.shape[3]
+    parts = wide.shape[1] // chunk
+    deep = wide.shape[0] // gw.shape[0]
+    moves = (
+        (gw_in, gw, wide, gw_out),
+        (hidden_in, hidden, hidden, hidden_out),
+        (gf_in, gf, gf, gf_out),
+        (gb_in, gb, gb, gb_out),
+    )
+    loads = [pltpu.make_async_copy(moves[k][0], moves[k][1], load_sem.at[k]) for k in range(4)]
+    stores = [pltpu.make_async_copy(moves[k][2], moves[k][3], store_sem.at[k]) for k in range(4)]
+    for load in loads:
+        load.start()
+    for k in range(4):
+        loads[k].wait()
+        if k == 0:
+            for n in range(gw.shape[0]):
+                for m in range(gw.shape[1]):
+                    top, l = n * deep + m // parts * GROUP, m % parts
+                    wide[top : top + GROUP, l * chunk : (l + 1) * chunk] = gw[n, m].astype(F32)
+        stores[k].start()
+    for copy in stores:
         copy.wait()
 
 
@@ -280,17 +319,16 @@
     dma = pltpu.SemaphoreType.DMA
     any_spec = pl.BlockSpec(memory_space=pl.ANY)
     hbm = pl.BlockSpec(memory_space=pltpu.HBM)
-    vmem = pl.BlockSpec(memory_space=pltpu.VMEM)
     hidden, gf, gw, gb = pl.pallas_call(
         functools.partial(kernel, n_row, n_col, inner, split),
         out_shape=(
             jax.ShapeDtypeStruct((own_rows, width), BF16),
             jax.ShapeDtypeStruct((rows, feat), BF16),
-            jax.ShapeDtypeStruct((feat, width), F32),
+            jax.ShapeDtypeStruct((split, n_col, GROUP, chunk), BF16),
             jax.ShapeDtypeStruct((1, width), F32),
         ),
         in_specs=[hbm] * 5 + [pl.BlockSpec(memory_space=pltpu.SMEM), hbm],
-        out_specs=(any_spec, any_spec, vmem, vmem),
+        out_specs=(any_spec,) * 4,
         scratch_shapes=[
             pltpu.VMEM((source, feat), BF16),
             pltpu.VMEM((feat, width), BF16),
@@ -302,17 +340,19 @@
             pltpu.VMEM((feat, target), BF16),
             pltpu.VMEM((n_row, own_rows, width), BF16),
             pltpu.VMEM((target, width), BF16),
-            pltpu.VMEM((outer, inner, feat, rows), BF16),
-            pltpu.VMEM((outer, inner, feat, rows), BF16),
+            pltpu.VMEM((inner, outer, feat, rows), BF16),
+            pltpu.VMEM((inner, outer, feat, rows), BF16),
             pltpu.VMEM((outer, feat, rows), BF16),
             pltpu.VMEM((outer, feat, rows), BF16),
             pltpu.VMEM((n_col, GROUP, chunk), BF16),
             pltpu.VMEM((n_col, GROUP, chunk), BF16),
             pltpu.VMEM((split, n_col, GROUP, chunk), BF16),
-            pltpu.VMEM((n_col, 1, width), F32),
+            pltpu.VMEM((inner, 1, width), F32),
+            pltpu.VMEM((outer, 1, width), F32),
+            pltpu.VMEM((1, width), F32),
             pltpu.VMEM((rows, feat), BF16),
             pltpu.SMEM(tile_index.shape, jnp.int32),
-            dma((6,)), dma((2,)),
+            dma((6,)), dma((5,)),
             dma((n_col,)), dma((n_col,)),
             dma((n_row,)), dma((n_row,)),
             dma((n_row,)), dma((n_row,)),
@@ -322,6 +362,7 @@
             dma((n_col,)), dma((n_col,)),
             dma((n_col,)), dma((n_col,)),
             dma((1,)), dma((1,)),
+            dma((outer,)), dma((outer,)),
         ],
         compiler_params=pltpu.CompilerParams(
             collective_id=0, has_side_effects=True, vmem_limit_bytes=60 * 1024 * 1024
@@ -335,10 +376,23 @@
     results = (hidden, gf, gw, gb)
     hidden, gf, gw, gb = pl.pallas_call(
         hand_over,
-        out_shape=tuple(jax.ShapeDtypeStruct(value.shape, value.dtype) for value in results),
+        out_shape=(
+            jax.ShapeDtypeStruct(hidden.shape, BF16),
+            jax.ShapeDtypeStruct(gf.shape, BF16),
+            jax.ShapeDtypeStruct((feat, width), F32),
+            jax.ShapeDtypeStruct(gb.shape, F32),
+        ),
         in_specs=[any_spec] * 4,
         out_specs=(any_spec,) * 4,
-        scratch_shapes=[dma((4,))],
+        scratch_shapes=[
+            pltpu.VMEM(hidden.shape, BF16),
+            pltpu.VMEM(gf.shape, BF16),
+            pltpu.VMEM(gw.shape, BF16),
+            pltpu.VMEM((feat, width), F32),
+            pltpu.VMEM(gb.shape, F32),
+            dma((4,)),
+            dma((4,)),
+        ],
         compiler_params=pltpu.CompilerParams(vmem_limit_bytes=60 * 1024 * 1024),
     )(*results)
     return hidden, gf, gw, gb.reshape(width)

time: 48.8 us -> 34.8 us (0.71)
  Pallas kernels: 47.3 us -> 33.4 us
    pallas_call x1, Pallas kernels: 14.1 us -> 1.74 us  [local(): pl.pallas_call(hand_over, out_shape=(jax.ShapeDtypeStruct(hidden.shape, B...]
    pallas_call x1, Pallas kernels: 33.2 us -> 31.7 us  [local(): pl.pallas_call(functools.partial(kernel, n_row, n_col, inner, split), out...]
where the time goes in v3:
time: 34.8 us; the launch traced here: 34.7 us
  Pallas kernels  33.4 us (96%)
  between operations  1.29 us (4%)
    pallas_call x1, Pallas kernels, local(): pl.pallas_call(functools.partial(kernel, n_row, n_col, inner, split), out...  31.7 us
    pallas_call x1, Pallas kernels, local(): pl.pallas_call(hand_over, out_shape=(jax.ShapeDtypeStruct(hidden.shape, B...  1.74 us

profile of v3, /device:TPU:0, one launch (start us, length us, event | category | flops | bytes accessed | tf_op | source)
XLA Modules:
  0.0 34.7 jit_solution(3397998410634933739)
XLA Ops:
  1.3 31.7 %shard_map.102 = (bf16[128,512]{1,0:T(8,128)(2,1)}, bf16[128,128]{1,0:T(8,128)(2,1)}, bf16[2,16,16,128]{3,2,1,0:T(8,128)(2,1)}, f32[1,512]{1,0:T(1,128)}) custom-call(bf16[128,128]{1,0:T(8,128)(2,1)} %features.1, bf16[128,512]{1,0:T(8,128)(2,1)} %weight.1, f32[1,512]{1,0:T(1,128)} %bitcast.2, bf16[1,1,16,128,128]{4,3,2,1,0:T(8,128)(2,1)} %tiles_in.1, ...), custom_call_target="tpu_custom_call" | custom-call | flops 369098752 | bytes 917504 | tf_op jit(solution)/shard_map/pallas_call | solution.py:322
  32.9 1.7 %shard_map.103 = (bf16[128,512]{1,0:T(8,128)(2,1)}, bf16[128,128]{1,0:T(8,128)(2,1)}, f32[128,512]{1,0:T(8,128)}, f32[1,512]{1,0:T(1,128)}) custom-call(bf16[128,512]{1,0:T(8,128)(2,1)} %get-tuple-element.12.hidden_in, bf16[128,128]{1,0:T(8,128)(2,1)} %get-tuple-element.13.gf_in, bf16[2,16,16,128]{3,2,1,0:T(8,128)(2,1)} %get-tuple-element.14.gw_in, ...), custom_call_target="tpu_custom_call" | custom-call | tf_op jit(solution)/shard_map/pallas_call | solution.py:377

commit v4 on v3

--- a/solution.py
+++ b/solution.py
@@ -24,13 +24,13 @@
 
 
 def kernel(
-    n_row, n_col, inner, split,
+    n_row, n_col, inner,
     features, weight, bias, tiles_in, index_in, count, cotangent,
     hidden_out, gf_out, gw_out, gb_out,
     x, w, b, tiles, adj, cot, hpart, hts, hid, dpre,
-    ssend, srecv, zsend, zrecv, gsend, grecv, gfull, bparts, bouter, gb, gf, index,
+    ssend, srecv, zsend, zrecv, gsend, grecv, gmid, gouter, gfull, bparts, bouter, gb, gf, index,
     load_sem, store_sem, x_send, x_recv, c_send, c_recv, h_send, h_recv,
-    s_send, s_recv, z_send, z_recv, g_send, g_recv, a_send, a_recv, b_send, b_recv, p_send, p_recv, d_send, d_recv,
+    s_send, s_recv, z_send, z_recv, g_send, g_recv, m_send, m_recv, a_send, a_recv, b_send, b_recv, p_send, p_recv, d_send, d_recv,
 ):
     r = lax.axis_index("row")
     c = lax.axis_index("col")
@@ -79,11 +79,13 @@
         load.start()
 
     barrier = pltpu.get_barrier_semaphore()
-    for d in range(1, n_col):
-        pl.semaphore_signal(barrier, inc=1, device_id=(r, lax.rem(c + d, n_col)), device_id_type=MESH)
+    for d in range(1, outer):
+        pl.semaphore_signal(barrier, inc=1, device_id=(r, col_of(d, 0)), device_id_type=MESH)
+    for q in range(1, inner):
+        pl.semaphore_signal(barrier, inc=1, device_id=(r, col_of(0, q)), device_id_type=MESH)
     for d in range(1, n_row):
         pl.semaphore_signal(barrier, inc=1, device_id=(lax.rem(r + d, n_row), c), device_id_type=MESH)
-    pl.semaphore_wait(barrier, n_col + n_row - 2)
+    pl.semaphore_wait(barrier, outer + inner + n_row - 3)
 
     pending = []
 
@@ -129,14 +131,16 @@
         adj[row, column] = jnp.where(slot >= 0, tile, jnp.zeros_like(tile))
         return carry
 
-    lax.fori_loop(0, tile_rows * tile_cols, place, 0)
-
-    for d in nearest_first(outer):
+    places = tile_rows * tile_cols
+    piece = places // outer
+    for m, d in enumerate(nearest_first(outer)):
+        lax.fori_loop(m * piece, (m + 1) * piece, place, 0)
         source = spot_of(d, 0)
         wait_x(source)
         for q in range(1, inner):
             send_x(number, source, col_of(0, q))
             number += 1
+    lax.fori_loop((outer - 1) * piece, places, place, 0)
     span = inner * rows
     partial = None
     for d in [0] + nearest_first(outer):
@@ -174,18 +178,16 @@
     store_h = pltpu.make_async_copy(hid.at[r], hidden_out, store_sem.at[0])
     store_h.start()
 
-    half = lax.rem(r, split)
-    deep = hts.shape[0] // split
-    gw = jnp.dot(hts[pl.ds(pl.multiple_of(half * deep, deep), deep), :], dpre[...], preferred_element_type=F32).astype(BF16)
-    chunk = gsend.shape[2]
+    gw = jnp.dot(hts[...], dpre[...], preferred_element_type=F32).astype(BF16)
+    chunk = gsend.shape[3]
     parts = width // chunk
     for k in range(n_col):
         g, l = k // parts, k % parts
-        gsend[k] = gw[g * GROUP : (g + 1) * GROUP, l * chunk : (l + 1) * chunk]
-    grecv[c] = gsend[c]
-    for d in range(1, n_col):
-        to = lax.rem(c + d, n_col)
-        send(remote(gsend.at[to], grecv.at[c], g_send.at[d], g_recv.at[c], (r, to)))
+        gsend[k // outer, k % outer] = gw[g * GROUP : (g + 1) * GROUP, l * chunk : (l + 1) * chunk]
+    for q in range(1, inner):
+        at = lax.rem(lo + q, inner)
+        send(remote(gsend.at[at], grecv.at[lo], g_send.at[q], g_recv.at[lo], (r, hi * inner + at)))
+    grecv[lo] = gsend[lo]
 
     gt = lax.dot_general(w[...], dpre[...], (((1,), (1,)), ((), ())), preferred_element_type=F32).astype(BF16)
     order = nearest_first(outer) + [0]
@@ -205,29 +207,19 @@
         at = lax.rem(lo + q, inner)
         send(remote(bparts.at[lo], bparts.at[lo], b_send.at[q], b_recv.at[lo], (r, hi * inner + at)))
 
-    for d in range(1, n_col):
-        source = lax.rem(c + d, n_col)
-        remote(gsend.at[0], grecv.at[source], g_send.at[0], g_recv.at[source], (r, c)).wait_recv()
+    for q in range(1, inner):
+        at = lax.rem(lo + q, inner)
+        remote(gsend.at[0], grecv.at[at], g_send.at[0], g_recv.at[at], (r, c)).wait_recv()
     total = grecv[0].astype(F32)
-    for k in range(1, n_col):
+    for k in range(1, inner):
         total = total + grecv[k].astype(F32)
-    gfull[half, c] = total.astype(BF16)
-    for d in range(1, n_col):
-        to = lax.rem(c + d, n_col)
-        send(remote(gfull.at[half, c], gfull.at[half, c], a_send.at[d], a_recv.at[c], (r, to)))
-
-    for q in range(1, inner):
-        at = lax.rem(lo + q, inner)
-        remote(bparts.at[at], bparts.at[at], b_send.at[0], b_recv.at[at], (r, c)).wait_recv()
-    bias_sum = bparts[0]
-    for q in range(1, inner):
-        bias_sum = bias_sum + bparts[q]
-    bouter[hi] = bias_sum
+    gmid[...] = total.astype(BF16)
     for d in range(1, outer):
         to = lax.rem(hi + d, outer)
-        send(remote(bouter.at[hi], bouter.at[hi], d_send.at[d], d_recv.at[hi], (r, to * inner + lo)))
-    own_sum = None
-    for n, d in enumerate(order):
+        send(remote(gmid.at[to], gouter.at[hi], m_send.at[d], m_recv.at[hi], (r, to * inner + lo)))
+    gouter[hi] = gmid[hi]
+
+    def pass_on(n, d):
         if n % portion == 0:
             run, m = pl.ds(n, portion), n // portion
             for q in range(1, inner):
@@ -237,12 +229,41 @@
         for q in range(1, inner):
             part = part + srecv[lax.rem(b_at + q, inner), n].astype(F32)
         if d:
-            to = lax.rem(a + d, outer)
             zsend[d] = part.astype(BF16)
-            send(remote(zsend.at[d], zrecv.at[a], z_send.at[d], z_recv.at[a], (r, col_at(to, b_at))))
-        else:
-            own_sum = part
-    sent()
+            to = col_at(lax.rem(a + d, outer), b_at)
+            send(remote(zsend.at[d], zrecv.at[a], z_send.at[d], z_recv.at[a], (r, to)))
+        return part
+
+    for n in range(portion):
+        pass_on(n, order[n])
+    for d in range(1, outer):
+        source = lax.rem(hi + d, outer)
+        remote(gmid.at[0], gouter.at[source], m_send.at[0], m_recv.at[source], (r, c)).wait_recv()
+    total = gouter[0].astype(F32)
+    for k in range(1, outer):
+        total = total + gouter[k].astype(F32)
+    gfull[lo, hi] = total.astype(BF16)
+    for d in range(1, outer):
+        to = lax.rem(hi + d, outer)
+        send(remote(gfull.at[lo, hi], gfull.at[lo, hi], a_send.at[d], a_recv.at[hi], (r, to * inner + lo)))
+    for n in range(portion, outer):
+        own_sum = pass_on(n, order[n])
+    for q in range(1, inner):
+        at = lax.rem(lo + q, inner)
+        remote(bparts.at[at], bparts.at[at], b_send.at[0], b_recv.at[at], (r, c)).wait_recv()
+    bias_sum = bparts[0]
+    for q in range(1, inner):
+        bias_sum = bias_sum + bparts[q]
+    bouter[hi] = bias_sum
+    for d in range(1, outer):
+        to = lax.rem(hi + d, outer)
+        send(remote(bouter.at[hi], bouter.at[hi], d_send.at[d], d_recv.at[hi], (r, to * inner + lo)))
+    for d in range(1, outer):
+        source = lax.rem(hi + d, outer)
+        remote(gfull.at[lo, source], gfull.at[lo, source], a_send.at[0], a_recv.at[source], (r, c)).wait_recv()
+    for q in range(1, inner):
+        at = lax.rem(lo + q, inner)
+        send(remote(gfull.at[lo], gfull.at[lo], p_send.at[q], p_recv.at[lo], (r, hi * inner + at)))
     for d in range(1, outer):
         source = lax.rem(hi + d, outer)
         remote(bouter.at[source], bouter.at[source], d_send.at[0], d_recv.at[source], (r, c)).wait_recv()
@@ -258,23 +279,17 @@
         stores.append(copy)
 
     store(gb, gb_out, 1)
-    for d in range(1, n_col):
-        source = lax.rem(c + d, n_col)
-        remote(gfull.at[half, source], gfull.at[half, source], a_send.at[0], a_recv.at[source], (r, c)).wait_recv()
-    if split == 2:
-        partner = r + 1 - 2 * half
-        send(remote(gfull.at[half], gfull.at[half], p_send.at[0], p_recv.at[0], (partner, c)))
-    store(gfull.at[half], gw_out.at[half], 2)
     for d in nearest_first(outer):
         source = lax.rem(a + d, outer)
         remote(zsend.at[0], zrecv.at[source], z_send.at[0], z_recv.at[source], (r, c)).wait_recv()
         own_sum = own_sum + zrecv[source].astype(F32)
     gf[...] = own_sum.T.astype(BF16)
-    store(gf, gf_out, 3)
-    if split == 2:
-        remote(gfull.at[1 - half], gfull.at[1 - half], p_send.at[0], p_recv.at[0], (r, c)).wait_recv()
-        store(gfull.at[1 - half], gw_out.at[1 - half], 4)
+    store(gf, gf_out, 2)
     sent()
+    for q in range(1, inner):
+        at = lax.rem(lo + q, inner)
+        remote(gfull.at[at], gfull.at[at], p_send.at[0], p_recv.at[at], (r, c)).wait_recv()
+    store(gfull, gw_out, 3)
     for copy in stores:
         copy.wait()
 
@@ -282,7 +297,6 @@
 def hand_over(hidden_in, gf_in, gw_in, gb_in, hidden_out, gf_out, gw_out, gb_out, hidden, gf, gw, wide, gb, load_sem, store_sem):
     chunk = gw.shape[3]
     parts = wide.shape[1] // chunk
-    deep = wide.shape[0] // gw.shape[0]
     moves = (
         (gw_in, gw, wide, gw_out),
         (hidden_in, hidden, hidden, hidden_out),
@@ -298,7 +312,8 @@
         if k == 0:
             for n in range(gw.shape[0]):
                 for m in range(gw.shape[1]):
-                    top, l = n * deep + m // parts * GROUP, m % parts
+                    number = n * gw.shape[1] + m
+                    top, l = number // parts * GROUP, number % parts
                     wide[top : top + GROUP, l * chunk : (l + 1) * chunk] = gw[n, m].astype(F32)
         stores[k].start()
     for copy in stores:
@@ -314,17 +329,15 @@
     target = n_row * own_rows
     source = n_col * rows
     chunk = feat * width // (GROUP * n_col)
-    split = 2 if n_row % 2 == 0 and chunk % 256 == 0 else 1
-    chunk = chunk // split
     dma = pltpu.SemaphoreType.DMA
     any_spec = pl.BlockSpec(memory_space=pl.ANY)
     hbm = pl.BlockSpec(memory_space=pltpu.HBM)
     hidden, gf, gw, gb = pl.pallas_call(
-        functools.partial(kernel, n_row, n_col, inner, split),
+        functools.partial(kernel, n_row, n_col, inner),
         out_shape=(
             jax.ShapeDtypeStruct((own_rows, width), BF16),
             jax.ShapeDtypeStruct((rows, feat), BF16),
-            jax.ShapeDtypeStruct((split, n_col, GROUP, chunk), BF16),
+            jax.ShapeDtypeStruct((inner, outer, GROUP, chunk), BF16),
             jax.ShapeDtypeStruct((1, width), F32),
         ),
         in_specs=[hbm] * 5 + [pl.BlockSpec(memory_space=pltpu.SMEM), hbm],
@@ -344,24 +357,27 @@
             pltpu.VMEM((inner, outer, feat, rows), BF16),
             pltpu.VMEM((outer, feat, rows), BF16),
             pltpu.VMEM((outer, feat, rows), BF16),
-            pltpu.VMEM((n_col, GROUP, chunk), BF16),
-            pltpu.VMEM((n_col, GROUP, chunk), BF16),
-            pltpu.VMEM((split, n_col, GROUP, chunk), BF16),
+            pltpu.VMEM((inner, outer, GROUP, chunk), BF16),
+            pltpu.VMEM((inner, outer, GROUP, chunk), BF16),
+            pltpu.VMEM((outer, GROUP, chunk), BF16),
+            pltpu.VMEM((outer, GROUP, chunk), BF16),
+            pltpu.VMEM((inner, outer, GROUP, chunk), BF16),
             pltpu.VMEM((inner, 1, width), F32),
             pltpu.VMEM((outer, 1, width), F32),
             pltpu.VMEM((1, width), F32),
             pltpu.VMEM((rows, feat), BF16),
             pltpu.SMEM(tile_index.shape, jnp.int32),
-            dma((6,)), dma((5,)),
+            dma((6,)), dma((4,)),
             dma((n_col,)), dma((n_col,)),
             dma((n_row,)), dma((n_row,)),
             dma((n_row,)), dma((n_row,)),
             dma((outer, inner)), dma((outer, inner)),
             dma((outer,)), dma((outer,)),
-            dma((n_col,)), dma((n_col,)),
-            dma((n_col,)), dma((n_col,)),
-            dma((n_col,)), dma((n_col,)),
-            dma((1,)), dma((1,)),
+            dma((inner,)), dma((inner,)),
+            dma((outer,)), dma((outer,)),
+            dma((outer,)), dma((outer,)),
+            dma((inner,)), dma((inner,)),
+            dma((inner,)), dma((inner,)),
             dma((outer,)), dma((outer,)),
         ],
         compiler_params=pltpu.CompilerParams(

time: 34.8 us -> 36.4 us (1.046)
  Pallas kernels: 33.4 us -> 34.9 us
    pallas_call x1, Pallas kernels: 31.7 us -> 33.2 us  [local(): pl.pallas_call(functools.partial(kernel, n_row, n_col, inner), out_shape=...]
where the time goes in v4:
time: 36.4 us; the launch traced here: 36.2 us
  Pallas kernels  34.9 us (96%)
  between operations  1.29 us (4%)
    pallas_call x1, Pallas kernels, local(): pl.pallas_call(functools.partial(kernel, n_row, n_col, inner), out_shape=...  33.2 us
    pallas_call x1, Pallas kernels, local(): pl.pallas_call(hand_over, out_shape=(jax.ShapeDtypeStruct(hidden.shape, B...  1.74 us

profile of v4, /device:TPU:0, one launch (start us, length us, event | category | flops | bytes accessed | tf_op | source)
XLA Modules:
  0.0 36.2 jit_solution(6766766373085766029)
XLA Ops:
  1.3 33.2 %shard_map.102 = (bf16[128,512]{1,0:T(8,128)(2,1)}, bf16[128,128]{1,0:T(8,128)(2,1)}, bf16[4,4,16,256]{3,2,1,0:T(8,128)(2,1)}, f32[1,512]{1,0:T(1,128)}) custom-call(bf16[128,128]{1,0:T(8,128)(2,1)} %features.1, bf16[128,512]{1,0:T(8,128)(2,1)} %weight.1, f32[1,512]{1,0:T(1,128)} %bitcast.2, bf16[1,1,16,128,128]{4,3,2,1,0:T(8,128)(2,1)} %tiles_in.1, ...), custom_call_target="tpu_custom_call" | custom-call | flops 369098752 | bytes 917504 | tf_op jit(solution)/shard_map/pallas_call | solution.py:335
  34.5 1.7 %shard_map.103 = (bf16[128,512]{1,0:T(8,128)(2,1)}, bf16[128,128]{1,0:T(8,128)(2,1)}, f32[128,512]{1,0:T(8,128)}, f32[1,512]{1,0:T(1,128)}) custom-call(bf16[128,512]{1,0:T(8,128)(2,1)} %get-tuple-element.12.hidden_in, bf16[128,128]{1,0:T(8,128)(2,1)} %get-tuple-element.13.gf_in, bf16[4,4,16,256]{3,2,1,0:T(8,128)(2,1)} %get-tuple-element.14.gw_in, ...), custom_call_target="tpu_custom_call" | custom-call | tf_op jit(solution)/shard_map/pallas_call | solution.py:393

commit v5 on v3

--- a/solution.py
+++ b/solution.py
@@ -129,14 +129,16 @@
         adj[row, column] = jnp.where(slot >= 0, tile, jnp.zeros_like(tile))
         return carry
 
-    lax.fori_loop(0, tile_rows * tile_cols, place, 0)
-
-    for d in nearest_first(outer):
+    places = tile_rows * tile_cols
+    piece = places // outer
+    for m, d in enumerate(nearest_first(outer)):
+        lax.fori_loop(m * piece, (m + 1) * piece, place, 0)
         source = spot_of(d, 0)
         wait_x(source)
         for q in range(1, inner):
             send_x(number, source, col_of(0, q))
             number += 1
+    lax.fori_loop((outer - 1) * piece, places, place, 0)
     span = inner * rows
     partial = None
     for d in [0] + nearest_first(outer):
@@ -162,7 +164,6 @@
     hb = h.astype(BF16)
     hts[...] = h.T.astype(BF16)
 
-    bias_sum = jnp.zeros((1, width), F32)
     for k in range(n_row):
         part = hb[k * own_rows : (k + 1) * own_rows]
         pre = jnp.dot(part, w[...], preferred_element_type=F32) + b[...]
@@ -170,7 +171,6 @@
         hid[k] = (pre * sig).astype(BF16)
         grad = (cot[k].astype(F32) * (sig + pre * sig * (1.0 - sig))).astype(BF16)
         dpre[k * own_rows : (k + 1) * own_rows, :] = grad
-        bias_sum = bias_sum + jnp.sum(grad.astype(F32), axis=0, keepdims=True)
     store_h = pltpu.make_async_copy(hid.at[r], hidden_out, store_sem.at[0])
     store_h.start()
 
@@ -200,7 +200,7 @@
             for q in range(1, inner):
                 at = lax.rem(b_at + q, inner)
                 send(remote(ssend.at[at, run], srecv.at[b_at, run], s_send.at[m, q], s_recv.at[m, b_at], (r, col_at(a, at))))
-    bparts[lo] = bias_sum
+    bparts[lo] = jnp.sum(dpre[...].astype(F32), axis=0, keepdims=True)
     for q in range(1, inner):
         at = lax.rem(lo + q, inner)
         send(remote(bparts.at[lo], bparts.at[lo], b_send.at[q], b_recv.at[lo], (r, hi * inner + at)))

time: 34.8 us -> 34.9 us (level)
  no operation moved by 1% of the time
where the time goes in v5:
time: 34.9 us; the launch traced here: 34.7 us
  Pallas kernels  33.4 us (96%)
  between operations  1.29 us (4%)
    pallas_call x1, Pallas kernels, local(): pl.pallas_call(functools.partial(kernel, n_row, n_col, inner, split), out...  31.7 us
    pallas_call x1, Pallas kernels, local(): pl.pallas_call(hand_over, out_shape=(jax.ShapeDtypeStruct(hidden.shape, B...  1.74 us

profile of v5, /device:TPU:0, one launch (start us, length us, event | category | flops | bytes accessed | tf_op | source)
XLA Modules:
  0.0 34.7 jit_solution(5370517416466454683)
XLA Ops:
  1.3 31.7 %shard_map.102 = (bf16[128,512]{1,0:T(8,128)(2,1)}, bf16[128,128]{1,0:T(8,128)(2,1)}, bf16[2,16,16,128]{3,2,1,0:T(8,128)(2,1)}, f32[1,512]{1,0:T(1,128)}) custom-call(bf16[128,128]{1,0:T(8,128)(2,1)} %features.1, bf16[128,512]{1,0:T(8,128)(2,1)} %weight.1, f32[1,512]{1,0:T(1,128)} %bitcast.2, bf16[1,1,16,128,128]{4,3,2,1,0:T(8,128)(2,1)} %tiles_in.1, ...), custom_call_target="tpu_custom_call" | custom-call | flops 369098752 | bytes 917504 | tf_op jit(solution)/shard_map/pallas_call | solution.py:322
  33.0 1.7 %shard_map.103 = (bf16[128,512]{1,0:T(8,128)(2,1)}, bf16[128,128]{1,0:T(8,128)(2,1)}, f32[128,512]{1,0:T(8,128)}, f32[1,512]{1,0:T(1,128)}) custom-call(bf16[128,512]{1,0:T(8,128)(2,1)} %get-tuple-element.12.hidden_in, bf16[128,128]{1,0:T(8,128)(2,1)} %get-tuple-element.13.gf_in, bf16[2,16,16,128]{3,2,1,0:T(8,128)(2,1)} %get-tuple-element.14.gw_in, ...), custom_call_target="tpu_custom_call" | custom-call | tf_op jit(solution)/shard_map/pallas_call | solution.py:377

commit v6 on v5

--- a/solution.py
+++ b/solution.py
@@ -314,7 +314,7 @@
     target = n_row * own_rows
     source = n_col * rows
     chunk = feat * width // (GROUP * n_col)
-    split = 2 if n_row % 2 == 0 and chunk % 256 == 0 else 1
+    split = 1
     chunk = chunk // split
     dma = pltpu.SemaphoreType.DMA
     any_spec = pl.BlockSpec(memory_space=pl.ANY)

time: 34.9 us -> 36.8 us (1.054)
  Pallas kernels: 33.4 us -> 35.4 us
    pallas_call x1, Pallas kernels: 31.7 us -> 33.6 us  [local(): pl.pallas_call(functools.partial(kernel, n_row, n_col, inner, split), out...]
where the time goes in v6:
time: 36.8 us; the launch traced here: 36.6 us
  Pallas kernels  35.4 us (96%)
  between operations  1.29 us (4%)
    pallas_call x1, Pallas kernels, local(): pl.pallas_call(functools.partial(kernel, n_row, n_col, inner, split), out...  33.6 us
    pallas_call x1, Pallas kernels, local(): pl.pallas_call(hand_over, out_shape=(jax.ShapeDtypeStruct(hidden.shape, B...  1.74 us

profile of v6, /device:TPU:0, one launch (start us, length us, event | category | flops | bytes accessed | tf_op | source)
XLA Modules:
  0.0 36.6 jit_solution(14321331027506442960)
XLA Ops:
  1.3 33.6 %shard_map.102 = (bf16[128,512]{1,0:T(8,128)(2,1)}, bf16[128,128]{1,0:T(8,128)(2,1)}, bf16[1,16,16,256]{3,2,1,0:T(8,128)(2,1)}, f32[1,512]{1,0:T(1,128)}) custom-call(bf16[128,128]{1,0:T(8,128)(2,1)} %features.1, bf16[128,512]{1,0:T(8,128)(2,1)} %weight.1, f32[1,512]{1,0:T(1,128)} %bitcast.2, bf16[1,1,16,128,128]{4,3,2,1,0:T(8,128)(2,1)} %tiles_in.1, ...), custom_call_target="tpu_custom_call" | custom-call | flops 369098752 | bytes 917504 | tf_op jit(solution)/shard_map/pallas_call | solution.py:322
  34.9 1.7 %shard_map.103 = (bf16[128,512]{1,0:T(8,128)(2,1)}, bf16[128,128]{1,0:T(8,128)(2,1)}, f32[128,512]{1,0:T(8,128)}, f32[1,512]{1,0:T(1,128)}) custom-call(bf16[128,512]{1,0:T(8,128)(2,1)} %get-tuple-element.12.hidden_in, bf16[128,128]{1,0:T(8,128)(2,1)} %get-tuple-element.13.gf_in, bf16[1,16,16,256]{3,2,1,0:T(8,128)(2,1)} %get-tuple-element.14.gw_in, ...), custom_call_target="tpu_custom_call" | custom-call | tf_op jit(solution)/shard_map/pallas_call | solution.py:377

commit v7 on v5

--- a/solution.py
+++ b/solution.py
@@ -174,19 +174,6 @@
     store_h = pltpu.make_async_copy(hid.at[r], hidden_out, store_sem.at[0])
     store_h.start()
 
-    half = lax.rem(r, split)
-    deep = hts.shape[0] // split
-    gw = jnp.dot(hts[pl.ds(pl.multiple_of(half * deep, deep), deep), :], dpre[...], preferred_element_type=F32).astype(BF16)
-    chunk = gsend.shape[2]
-    parts = width // chunk
-    for k in range(n_col):
-        g, l = k // parts, k % parts
-        gsend[k] = gw[g * GROUP : (g + 1) * GROUP, l * chunk : (l + 1) * chunk]
-    grecv[c] = gsend[c]
-    for d in range(1, n_col):
-        to = lax.rem(c + d, n_col)
-        send(remote(gsend.at[to], grecv.at[c], g_send.at[d], g_recv.at[c], (r, to)))
-
     gt = lax.dot_general(w[...], dpre[...], (((1,), (1,)), ((), ())), preferred_element_type=F32).astype(BF16)
     order = nearest_first(outer) + [0]
     portion = max(1, outer // 2)
@@ -200,6 +187,19 @@
             for q in range(1, inner):
                 at = lax.rem(b_at + q, inner)
                 send(remote(ssend.at[at, run], srecv.at[b_at, run], s_send.at[m, q], s_recv.at[m, b_at], (r, col_at(a, at))))
+    half = lax.rem(r, split)
+    deep = hts.shape[0] // split
+    gw = jnp.dot(hts[pl.ds(pl.multiple_of(half * deep, deep), deep), :], dpre[...], preferred_element_type=F32).astype(BF16)
+    chunk = gsend.shape[2]
+    parts = width // chunk
+    for k in range(n_col):
+        g, l = k // parts, k % parts
+        gsend[k] = gw[g * GROUP : (g + 1) * GROUP, l * chunk : (l + 1) * chunk]
+    grecv[c] = gsend[c]
+    for d in range(1, n_col):
+        to = lax.rem(c + d, n_col)
+        send(remote(gsend.at[to], grecv.at[c], g_send.at[d], g_recv.at[c], (r, to)))
+
     bparts[lo] = jnp.sum(dpre[...].astype(F32), axis=0, keepdims=True)
     for q in range(1, inner):
         at = lax.rem(lo + q, inner)

time: 34.9 us -> 37.9 us (1.086)
  Pallas kernels: 33.4 us -> 36.5 us
    pallas_call x1, Pallas kernels: 31.7 us -> 34.8 us  [local(): pl.pallas_call(functools.partial(kernel, n_row, n_col, inner, split), out...]
where the time goes in v7:
time: 37.9 us; the launch traced here: 37.8 us
  Pallas kernels  36.5 us (96%)
  between operations  1.29 us (3%)
    pallas_call x1, Pallas kernels, local(): pl.pallas_call(functools.partial(kernel, n_row, n_col, inner, split), out...  34.8 us
    pallas_call x1, Pallas kernels, local(): pl.pallas_call(hand_over, out_shape=(jax.ShapeDtypeStruct(hidden.shape, B...  1.74 us

profile of v7, /device:TPU:0, one launch (start us, length us, event | category | flops | bytes accessed | tf_op | source)
XLA Modules:
  0.0 37.8 jit_solution(8251708513940047127)
XLA Ops:
  1.3 34.8 %shard_map.102 = (bf16[128,512]{1,0:T(8,128)(2,1)}, bf16[128,128]{1,0:T(8,128)(2,1)}, bf16[2,16,16,128]{3,2,1,0:T(8,128)(2,1)}, f32[1,512]{1,0:T(1,128)}) custom-call(bf16[128,128]{1,0:T(8,128)(2,1)} %features.1, bf16[128,512]{1,0:T(8,128)(2,1)} %weight.1, f32[1,512]{1,0:T(1,128)} %bitcast.2, bf16[1,1,16,128,128]{4,3,2,1,0:T(8,128)(2,1)} %tiles_in.1, ...), custom_call_target="tpu_custom_call" | custom-call | flops 369098752 | bytes 917504 | tf_op jit(solution)/shard_map/pallas_call | solution.py:322
  36.0 1.7 %shard_map.103 = (bf16[128,512]{1,0:T(8,128)(2,1)}, bf16[128,128]{1,0:T(8,128)(2,1)}, f32[128,512]{1,0:T(8,128)}, f32[1,512]{1,0:T(1,128)}) custom-call(bf16[128,512]{1,0:T(8,128)(2,1)} %get-tuple-element.12.hidden_in, bf16[128,128]{1,0:T(8,128)(2,1)} %get-tuple-element.13.gf_in, bf16[2,16,16,128]{3,2,1,0:T(8,128)(2,1)} %get-tuple-element.14.gw_in, ...), custom_call_target="tpu_custom_call" | custom-call | tf_op jit(solution)/shard_map/pallas_call | solution.py:377
